TPU v7x, 1024 devices: a whole 4x4x32 slice. The times are simulated.
1024 devices in a mesh: row: 32 (over z_hi, x, y), col: 32 (over z_lo, core).
Axes of the slice: x: 4, y: 4, z: 32 (z_hi: 2, z_lo: 16; z = z_hi * 16 + z_lo), core: 2. Of those that a mesh axis runs over, the one named last changes fastest.
Arguments:
- p_blocks: bfloat16 [32, 32, 3, 128, 128], P('row', 'col'), may hold values from -1.5 to 1.5
- p_rows: int32 [32, 32, 3], P('row', 'col'), may hold values from 0 to 12, as said below
- p_cols: int32 [32, 32, 3], P('row', 'col'), may hold values from 0 to 12
- p_count: int32 [32, 32], P('row', 'col'), may hold values from 2 to 3, as said below
- kept_rows: int32 [32, 32, 6], P('row', 'col'), may hold values from 0 to 12, as said below
- kept_cols: int32 [32, 32, 6], P('row', 'col'), may hold values from 0 to 12
Outputs:
- square_blocks: float32 [32, 32, 6, 128, 128], P('row', 'col')
Inputs may be any that keep to these rules, and one draw needn't show every extreme that they name: `p_rows`: within one device tile the used slots name distinct blocks. `p_count`: some device tile uses all 3 slots. `kept_rows`: within one device tile the kept blocks are distinct.
All inputs are finite; a program needn't handle non-finite values.
Results may differ from a plain program's by a relative error of at most 0.0003.
Values may be sent and summed in bfloat16 or wider, within the bound.
A program may use at most 32 MiB of HBM per device.

v0:
```python
import jax
import jax.numpy as jnp
from jax import lax
from jax.sharding import PartitionSpec as P

TBC = 13


def as_sent(value):

    def short(part):
        return part.astype(jnp.bfloat16) if part.dtype == jnp.float32 else part

    return jax.tree.map(short, value)


def passed_along(value, axis, by):
    size = lax.axis_size(axis)
    return lax.ppermute(value, axis, [(i, (i + by) % size) for i in range(size)])


def pick_tree(flag, arrived, current):
    return jax.tree.map(
        lambda new_part, old_part: jnp.where(flag, new_part, old_part), arrived, current
    )


def body(p_blocks, p_rows, p_cols, p_count, kept_rows, kept_cols):
    n_row = lax.axis_size("row")
    n_col = lax.axis_size("col")
    col_per_row = n_col // n_row
    row_index = lax.axis_index("row")
    col_index = lax.axis_index("col")
    slot_count = p_blocks.shape[2]
    is_valid = jnp.arange(slot_count, dtype=jnp.int32) < p_count[0, 0]
    blocks = jnp.where(is_valid[:, None, None], p_blocks[0, 0], jnp.zeros_like(p_blocks[0, 0]))
    slot_index = jnp.stack([p_rows[0, 0], p_cols[0, 0]])
    out_rows = kept_rows[0, 0]
    out_cols = kept_cols[0, 0]
    block_size = blocks.shape[-1]

    def contribute(total, left_side, right_side, inner_piece):
        left_blocks, left_index = left_side
        right_blocks, right_index = right_side
        right_rows = right_index[0] - inner_piece % col_per_row * TBC
        weights = (
            (left_index[0][None, :, None] == out_rows[:, None, None])
            & (right_index[1][None, None, :] == out_cols[:, None, None])
            & (left_index[1][None, :, None] == right_rows[None, None, :])
        ).astype(jnp.float32)
        products = jnp.einsum(
            "aik,bkj->abij", left_blocks, right_blocks, preferred_element_type=jnp.float32
        )
        return total + jnp.einsum(
            "oab,abij->oij", weights, products, precision=lax.Precision.HIGHEST
        )

    start = jnp.zeros((out_rows.shape[0], block_size, block_size), jnp.float32)
    left_side = (blocks, slot_index)
    right_side = (blocks, slot_index)
    left_amount = row_index * col_per_row
    for bit_number in range((n_col - 1).bit_length()):
        arrived = jax.tree.map(
            lambda part, own: part.astype(own.dtype),
            passed_along(as_sent(left_side), "col", -(1 << bit_number)),
            left_side,
        )
        left_side = pick_tree(left_amount >> bit_number & 1 == 1, arrived, left_side)
    right_amount = col_index // col_per_row
    for bit_number in range((n_row - 1).bit_length()):
        arrived = jax.tree.map(
            lambda part, own: part.astype(own.dtype),
            passed_along(as_sent(right_side), "row", -(1 << bit_number)),
            right_side,
        )
        right_side = pick_tree(right_amount >> bit_number & 1 == 1, arrived, right_side)

    def advance_step(step_number, state_now):
        total, left_now, right_now = state_now
        inner_piece = (row_index * col_per_row + col_index + step_number) % n_col
        total = contribute(total, left_now, right_now, inner_piece)
        left_next = jax.tree.map(
            lambda part, own: part.astype(own.dtype),
            passed_along(as_sent(left_now), "col", -1),
            left_now,
        )
        arrived = jax.tree.map(
            lambda part, own: part.astype(own.dtype),
            passed_along(as_sent(right_now), "row", -1),
            right_now,
        )
        right_next = pick_tree((col_index + step_number + 1) % col_per_row == 0, arrived, right_now)
        return (total, left_next, right_next)

    total, left_side, right_side = lax.fori_loop(
        0, n_col - 1, advance_step, (start, left_side, right_side)
    )
    last_piece = (row_index * col_per_row + col_index + n_col - 1) % n_col
    total = contribute(total, left_side, right_side, last_piece)
    return total[None, None]


def solution(mesh):
    placed = (
        P("row", "col", None, None, None),
        P("row", "col", None),
        P("row", "col", None),
        P("row", "col"),
        P("row", "col", None),
        P("row", "col", None),
    )
    return jax.shard_map(
        body,
        mesh=mesh,
        in_specs=placed,
        out_specs=P("row", "col", None, None, None),
        check_vma=False,
    )
```

profile of v0, /device:TPU:63, one launch (start us, length us, event | category | flops | bytes accessed | tf_op | source)
XLA Modules:
  0.0 1522.2 jit_solution(12152961791008437701)
XLA Ops:
  11.4 23.3 %collective-permute-done.19 = s32[2,3]{1,0:T(2,128)S(1)} collective-permute-done((s32[2,3]{1,0:T(2,128)S(1)}, s32[2,3]{1,0:T(2,128)S(1)}, u32[]{:S(2)}, u32[]{:S(2)}) %collective-permute-start.19) | collective-permute-done | bytes 56 | tf_op jit(solution)/shard_map/ppermute | solution.py:19
  43.0 40.8 %collective-permute-start.11 = (s32[2,3]{1,0:T(2,128)S(1)}, s32[2,3]{1,0:T(2,128)S(1)}, u32[]{:S(2)}, u32[]{:S(2)}) collective-permute-start(s32[2,3]{1,0:T(2,128)S(1)} %broadcast_select_fusion.16), channel_id=1, source_target_pairs={{0,28},{1,29},{2,30},{3,31},{4,0},{5,1},{6,2},{7,3},{8,4},{9,5},{1... | collective-permute-start | bytes 80 | tf_op jit(solution)/shard_map/ppermute | solution.py:19
  85.8 6.9 collective-permute-start.12
  92.7 15.9 %collective-permute-done.21 = s32[2,3]{1,0:T(2,128)S(1)} collective-permute-done((s32[2,3]{1,0:T(2,128)S(1)}, s32[2,3]{1,0:T(2,128)S(1)}, u32[]{:S(2)}, u32[]{:S(2)}) %collective-permute-start.21) | collective-permute-done | bytes 56 | tf_op jit(solution)/shard_map/ppermute | solution.py:19
  112.5 21.2 %collective-permute-done.22 = s32[2,3]{1,0:T(2,128)S(1)} collective-permute-done((s32[2,3]{1,0:T(2,128)S(1)}, s32[2,3]{1,0:T(2,128)S(1)}, u32[]{:S(2)}, u32[]{:S(2)}) %collective-permute-start.22) | collective-permute-done | bytes 56 | tf_op jit(solution)/shard_map/ppermute | solution.py:19
  133.7 17.9 %collective-permute-start.23 = (s32[2,3]{1,0:T(2,128)S(1)}, s32[2,3]{1,0:T(2,128)S(1)}, u32[]{:S(2)}, u32[]{:S(2)}) collective-permute-start(s32[2,3]{1,0:T(2,128)S(1)} %broadcast_select_fusion.13), channel_id=1, source_target_pairs={{0,512},{32,544},{64,576},{96,608},{128,640},{160,672},{192,704},{... | collective-permute-start | bytes 80 | tf_op jit(solution)/shard_map/ppermute | solution.py:19
  158.3 20.4 %collective-permute-start.6 = (bf16[3,128,128]{2,1,0:T(8,128)(2,1)S(1)}, bf16[3,128,128]{2,1,0:T(8,128)(2,1)S(1)}, u32[]{:S(2)}, u32[]{:S(2)}) collective-permute-start(bf16[3,128,128]{2,1,0:T(8,128)(2,1)S(1)} %broadcast_select_fusion.6), channel_id=1, source_target_pairs={{0,28},{1,29},{2,30},{3,31},{4,0},{5,1},{6,2},{7,3},{8,4},{9,5},{1... | collective-permute-start | bytes 294920 | tf_op jit(solution)/shard_map/ppermute | solution.py:19
  178.6 17.2 %collective-permute-done.15 = bf16[3,128,128]{2,1,0:T(8,128)(2,1)S(1)} collective-permute-done((bf16[3,128,128]{2,1,0:T(8,128)(2,1)S(1)}, bf16[3,128,128]{2,1,0:T(8,128)(2,1)S(1)}, u32[]{:S(2)}, u32[]{:S(2)}) %collective-permute-start.15) | collective-permute-done | bytes 98336 | tf_op jit(solution)/shard_map/ppermute | solution.py:19
  199.8 22.2 %collective-permute-done.16 = bf16[3,128,128]{2,1,0:T(8,128)(2,1)S(1)} collective-permute-done((bf16[3,128,128]{2,1,0:T(8,128)(2,1)S(1)}, bf16[3,128,128]{2,1,0:T(8,128)(2,1)S(1)}, u32[]{:S(2)}, u32[]{:S(2)}) %collective-permute-start.16) | collective-permute-done | bytes 98336 | tf_op jit(solution)/shard_map/ppermute | solution.py:19
  225.9 22.4 %collective-permute-done.17 = bf16[3,128,128]{2,1,0:T(8,128)(2,1)S(1)} collective-permute-done((bf16[3,128,128]{2,1,0:T(8,128)(2,1)S(1)}, bf16[3,128,128]{2,1,0:T(8,128)(2,1)S(1)}, u32[]{:S(2)}, u32[]{:S(2)}) %collective-permute-start.17) | collective-permute-done | bytes 98336 | tf_op jit(solution)/shard_map/ppermute | solution.py:19
  248.3 9.2 collective-permute-start.18
  257.5 14.5 collective-permute-done.18
  272.0 1247.5 %while.25 = (s32[]{:T(128)}, f32[6,128,128]{2,0,1:T(8,128)S(1)}, bf16[3,128,128]{2,1,0:T(8,128)(2,1)S(1)}, s32[2,3]{1,0:T(2,128)S(1)}, bf16[3,128,128]{2,1,0:T(8...) while((s32[]{:T(128)}, f32[6,128,128]{2,0,1:T(8,128)S(1)}, ...), condition=%wide.region_1.2_spmd.clone, body=%wide.region_0.1_spmd.clone.sunk | while | flops 48562324 | bytes 4522825 | solution.py:95
  272.0 29.2 %collective-permute-start = (bf16[3,128,128]{2,1,0:T(8,128)(2,1)S(1)}, bf16[3,128,128]{2,1,0:T(8,128)(2,1)S(1)}, u32[]{:S(2)}, u32[]{:S(2)}) collective-permute-start(bf16[3,128,128]{2,1,0:T(8,128)(2,1)S(1)} %copy.24), channel_id=1, source_target_pairs={{0,31},{1,0},{2,1},{3,2},{4,3},{5,4},{6,5},{7,6},{8,7},{9,8},{10,9... | collective-permute-start | bytes 294920 | tf_op jit(solution)/shard_map/while/body/eval_jaxpr/ppermute | solution.py:19
  309.0 26.8 %collective-permute-done.3 = s32[2,3]{1,0:T(2,128)S(1)} collective-permute-done((s32[2,3]{1,0:T(2,128)S(1)}, s32[2,3]{1,0:T(2,128)S(1)}, u32[]{:S(2)}, u32[]{:S(2)}) %collective-permute-start.3) | collective-permute-done | bytes 56 | tf_op jit(solution)/shard_map/while/body/eval_jaxpr/ppermute | solution.py:19
  346.0 23.6 %collective-permute-done.3 = s32[2,3]{1,0:T(2,128)S(1)} collective-permute-done((s32[2,3]{1,0:T(2,128)S(1)}, s32[2,3]{1,0:T(2,128)S(1)}, u32[]{:S(2)}, u32[]{:S(2)}) %collective-permute-start.3) | collective-permute-done | bytes 56 | tf_op jit(solution)/shard_map/while/body/eval_jaxpr/ppermute | solution.py:19
  369.6 9.9 collective-permute-start
  389.0 25.3 %collective-permute-done.3 = s32[2,3]{1,0:T(2,128)S(1)} collective-permute-done((s32[2,3]{1,0:T(2,128)S(1)}, s32[2,3]{1,0:T(2,128)S(1)}, u32[]{:S(2)}, u32[]{:S(2)}) %collective-permute-start.3) | collective-permute-done | bytes 56 | tf_op jit(solution)/shard_map/while/body/eval_jaxpr/ppermute | solution.py:19
  425.3 27.0 %collective-permute-done.3 = s32[2,3]{1,0:T(2,128)S(1)} collective-permute-done((s32[2,3]{1,0:T(2,128)S(1)}, s32[2,3]{1,0:T(2,128)S(1)}, u32[]{:S(2)}, u32[]{:S(2)}) %collective-permute-start.3) | collective-permute-done | bytes 56 | tf_op jit(solution)/shard_map/while/body/eval_jaxpr/ppermute | solution.py:19
  462.7 26.3 %collective-permute-done.3 = s32[2,3]{1,0:T(2,128)S(1)} collective-permute-done((s32[2,3]{1,0:T(2,128)S(1)}, s32[2,3]{1,0:T(2,128)S(1)}, u32[]{:S(2)}, u32[]{:S(2)}) %collective-permute-start.3) | collective-permute-done | bytes 56 | tf_op jit(solution)/shard_map/while/body/eval_jaxpr/ppermute | solution.py:19
  499.3 26.9 %collective-permute-done.3 = s32[2,3]{1,0:T(2,128)S(1)} collective-permute-done((s32[2,3]{1,0:T(2,128)S(1)}, s32[2,3]{1,0:T(2,128)S(1)}, u32[]{:S(2)}, u32[]{:S(2)}) %collective-permute-start.3) | collective-permute-done | bytes 56 | tf_op jit(solution)/shard_map/while/body/eval_jaxpr/ppermute | solution.py:19
  536.7 26.4 %collective-permute-done.3 = s32[2,3]{1,0:T(2,128)S(1)} collective-permute-done((s32[2,3]{1,0:T(2,128)S(1)}, s32[2,3]{1,0:T(2,128)S(1)}, u32[]{:S(2)}, u32[]{:S(2)}) %collective-permute-start.3) | collective-permute-done | bytes 56 | tf_op jit(solution)/shard_map/while/body/eval_jaxpr/ppermute | solution.py:19
  573.5 26.9 %collective-permute-done.3 = s32[2,3]{1,0:T(2,128)S(1)} collective-permute-done((s32[2,3]{1,0:T(2,128)S(1)}, s32[2,3]{1,0:T(2,128)S(1)}, u32[]{:S(2)}, u32[]{:S(2)}) %collective-permute-start.3) | collective-permute-done | bytes 56 | tf_op jit(solution)/shard_map/while/body/eval_jaxpr/ppermute | solution.py:19
  610.7 24.7 %collective-permute-done.3 = s32[2,3]{1,0:T(2,128)S(1)} collective-permute-done((s32[2,3]{1,0:T(2,128)S(1)}, s32[2,3]{1,0:T(2,128)S(1)}, u32[]{:S(2)}, u32[]{:S(2)}) %collective-permute-start.3) | collective-permute-done | bytes 56 | tf_op jit(solution)/shard_map/while/body/eval_jaxpr/ppermute | solution.py:19
  645.6 25.2 %collective-permute-done.3 = s32[2,3]{1,0:T(2,128)S(1)} collective-permute-done((s32[2,3]{1,0:T(2,128)S(1)}, s32[2,3]{1,0:T(2,128)S(1)}, u32[]{:S(2)}, u32[]{:S(2)}) %collective-permute-start.3) | collective-permute-done | bytes 56 | tf_op jit(solution)/shard_map/while/body/eval_jaxpr/ppermute | solution.py:19
  681.4 25.1 %collective-permute-done.3 = s32[2,3]{1,0:T(2,128)S(1)} collective-permute-done((s32[2,3]{1,0:T(2,128)S(1)}, s32[2,3]{1,0:T(2,128)S(1)}, u32[]{:S(2)}, u32[]{:S(2)}) %collective-permute-start.3) | collective-permute-done | bytes 56 | tf_op jit(solution)/shard_map/while/body/eval_jaxpr/ppermute | solution.py:19
  706.6 28.3 %collective-permute-start = (bf16[3,128,128]{2,1,0:T(8,128)(2,1)S(1)}, bf16[3,128,128]{2,1,0:T(8,128)(2,1)S(1)}, u32[]{:S(2)}, u32[]{:S(2)}) collective-permute-start(bf16[3,128,128]{2,1,0:T(8,128)(2,1)S(1)} %copy.24), channel_id=1, source_target_pairs={{0,31},{1,0},{2,1},{3,2},{4,3},{5,4},{6,5},{7,6},{8,7},{9,8},{10,9... | collective-permute-start | bytes 294920 | tf_op jit(solution)/shard_map/while/body/eval_jaxpr/ppermute | solution.py:19
  734.9 5.1 collective-permute-start.1
  745.9 32.9 %collective-permute-done.3 = s32[2,3]{1,0:T(2,128)S(1)} collective-permute-done((s32[2,3]{1,0:T(2,128)S(1)}, s32[2,3]{1,0:T(2,128)S(1)}, u32[]{:S(2)}, u32[]{:S(2)}) %collective-permute-start.3) | collective-permute-done | bytes 56 | tf_op jit(solution)/shard_map/while/body/eval_jaxpr/ppermute | solution.py:19
  789.1 24.7 %collective-permute-done.3 = s32[2,3]{1,0:T(2,128)S(1)} collective-permute-done((s32[2,3]{1,0:T(2,128)S(1)}, s32[2,3]{1,0:T(2,128)S(1)}, u32[]{:S(2)}, u32[]{:S(2)}) %collective-permute-start.3) | collective-permute-done | bytes 56 | tf_op jit(solution)/shard_map/while/body/eval_jaxpr/ppermute | solution.py:19
  824.0 28.6 %collective-permute-done.3 = s32[2,3]{1,0:T(2,128)S(1)} collective-permute-done((s32[2,3]{1,0:T(2,128)S(1)}, s32[2,3]{1,0:T(2,128)S(1)}, u32[]{:S(2)}, u32[]{:S(2)}) %collective-permute-start.3) | collective-permute-done | bytes 56 | tf_op jit(solution)/shard_map/while/body/eval_jaxpr/ppermute | solution.py:19
  863.0 26.3 %collective-permute-done.3 = s32[2,3]{1,0:T(2,128)S(1)} collective-permute-done((s32[2,3]{1,0:T(2,128)S(1)}, s32[2,3]{1,0:T(2,128)S(1)}, u32[]{:S(2)}, u32[]{:S(2)}) %collective-permute-start.3) | collective-permute-done | bytes 56 | tf_op jit(solution)/shard_map/while/body/eval_jaxpr/ppermute | solution.py:19
  899.7 25.3 %collective-permute-done.3 = s32[2,3]{1,0:T(2,128)S(1)} collective-permute-done((s32[2,3]{1,0:T(2,128)S(1)}, s32[2,3]{1,0:T(2,128)S(1)}, u32[]{:S(2)}, u32[]{:S(2)}) %collective-permute-start.3) | collective-permute-done | bytes 56 | tf_op jit(solution)/shard_map/while/body/eval_jaxpr/ppermute | solution.py:19
  935.3 23.7 %collective-permute-done.3 = s32[2,3]{1,0:T(2,128)S(1)} collective-permute-done((s32[2,3]{1,0:T(2,128)S(1)}, s32[2,3]{1,0:T(2,128)S(1)}, u32[]{:S(2)}, u32[]{:S(2)}) %collective-permute-start.3) | collective-permute-done | bytes 56 | tf_op jit(solution)/shard_map/while/body/eval_jaxpr/ppermute | solution.py:19
  970.1 29.3 %collective-permute-done.3 = s32[2,3]{1,0:T(2,128)S(1)} collective-permute-done((s32[2,3]{1,0:T(2,128)S(1)}, s32[2,3]{1,0:T(2,128)S(1)}, u32[]{:S(2)}, u32[]{:S(2)}) %collective-permute-start.3) | collective-permute-done | bytes 56 | tf_op jit(solution)/shard_map/while/body/eval_jaxpr/ppermute | solution.py:19
  1009.7 23.7 %collective-permute-done.3 = s32[2,3]{1,0:T(2,128)S(1)} collective-permute-done((s32[2,3]{1,0:T(2,128)S(1)}, s32[2,3]{1,0:T(2,128)S(1)}, u32[]{:S(2)}, u32[]{:S(2)}) %collective-permute-start.3) | collective-permute-done | bytes 56 | tf_op jit(solution)/shard_map/while/body/eval_jaxpr/ppermute | solution.py:19
  1046.2 29.6 %collective-permute-done.3 = s32[2,3]{1,0:T(2,128)S(1)} collective-permute-done((s32[2,3]{1,0:T(2,128)S(1)}, s32[2,3]{1,0:T(2,128)S(1)}, u32[]{:S(2)}, u32[]{:S(2)}) %collective-permute-start.3) | collective-permute-done | bytes 56 | tf_op jit(solution)/shard_map/while/body/eval_jaxpr/ppermute | solution.py:19
  1086.5 29.2 %collective-permute-done.3 = s32[2,3]{1,0:T(2,128)S(1)} collective-permute-done((s32[2,3]{1,0:T(2,128)S(1)}, s32[2,3]{1,0:T(2,128)S(1)}, u32[]{:S(2)}, u32[]{:S(2)}) %collective-permute-start.3) | collective-permute-done | bytes 56 | tf_op jit(solution)/shard_map/while/body/eval_jaxpr/ppermute | solution.py:19
  1126.1 29.4 %collective-permute-done.3 = s32[2,3]{1,0:T(2,128)S(1)} collective-permute-done((s32[2,3]{1,0:T(2,128)S(1)}, s32[2,3]{1,0:T(2,128)S(1)}, u32[]{:S(2)}, u32[]{:S(2)}) %collective-permute-start.3) | collective-permute-done | bytes 56 | tf_op jit(solution)/shard_map/while/body/eval_jaxpr/ppermute | solution.py:19
  1165.9 30.1 %collective-permute-done.3 = s32[2,3]{1,0:T(2,128)S(1)} collective-permute-done((s32[2,3]{1,0:T(2,128)S(1)}, s32[2,3]{1,0:T(2,128)S(1)}, u32[]{:S(2)}, u32[]{:S(2)}) %collective-permute-start.3) | collective-permute-done | bytes 56 | tf_op jit(solution)/shard_map/while/body/eval_jaxpr/ppermute | solution.py:19
  1206.3 32.4 %collective-permute-done.3 = s32[2,3]{1,0:T(2,128)S(1)} collective-permute-done((s32[2,3]{1,0:T(2,128)S(1)}, s32[2,3]{1,0:T(2,128)S(1)}, u32[]{:S(2)}, u32[]{:S(2)}) %collective-permute-start.3) | collective-permute-done | bytes 56 | tf_op jit(solution)/shard_map/while/body/eval_jaxpr/ppermute | solution.py:19
  1249.2 30.7 %collective-permute-done.3 = s32[2,3]{1,0:T(2,128)S(1)} collective-permute-done((s32[2,3]{1,0:T(2,128)S(1)}, s32[2,3]{1,0:T(2,128)S(1)}, u32[]{:S(2)}, u32[]{:S(2)}) %collective-permute-start.3) | collective-permute-done | bytes 56 | tf_op jit(solution)/shard_map/while/body/eval_jaxpr/ppermute | solution.py:19
  1290.3 32.0 %collective-permute-done.3 = s32[2,3]{1,0:T(2,128)S(1)} collective-permute-done((s32[2,3]{1,0:T(2,128)S(1)}, s32[2,3]{1,0:T(2,128)S(1)}, u32[]{:S(2)}, u32[]{:S(2)}) %collective-permute-start.3) | collective-permute-done | bytes 56 | tf_op jit(solution)/shard_map/while/body/eval_jaxpr/ppermute | solution.py:19
  1332.6 27.2 %collective-permute-done.3 = s32[2,3]{1,0:T(2,128)S(1)} collective-permute-done((s32[2,3]{1,0:T(2,128)S(1)}, s32[2,3]{1,0:T(2,128)S(1)}, u32[]{:S(2)}, u32[]{:S(2)}) %collective-permute-start.3) | collective-permute-done | bytes 56 | tf_op jit(solution)/shard_map/while/body/eval_jaxpr/ppermute | solution.py:19
  1370.1 33.8 %collective-permute-done.3 = s32[2,3]{1,0:T(2,128)S(1)} collective-permute-done((s32[2,3]{1,0:T(2,128)S(1)}, s32[2,3]{1,0:T(2,128)S(1)}, u32[]{:S(2)}, u32[]{:S(2)}) %collective-permute-start.3) | collective-permute-done | bytes 56 | tf_op jit(solution)/shard_map/while/body/eval_jaxpr/ppermute | solution.py:19
  1414.3 29.7 %collective-permute-done.3 = s32[2,3]{1,0:T(2,128)S(1)} collective-permute-done((s32[2,3]{1,0:T(2,128)S(1)}, s32[2,3]{1,0:T(2,128)S(1)}, u32[]{:S(2)}, u32[]{:S(2)}) %collective-permute-start.3) | collective-permute-done | bytes 56 | tf_op jit(solution)/shard_map/while/body/eval_jaxpr/ppermute | solution.py:19
  1454.4 26.4 %collective-permute-done.3 = s32[2,3]{1,0:T(2,128)S(1)} collective-permute-done((s32[2,3]{1,0:T(2,128)S(1)}, s32[2,3]{1,0:T(2,128)S(1)}, u32[]{:S(2)}, u32[]{:S(2)}) %collective-permute-start.3) | collective-permute-done | bytes 56 | tf_op jit(solution)/shard_map/while/body/eval_jaxpr/ppermute | solution.py:19
  1491.1 28.5 %collective-permute-done.3 = s32[2,3]{1,0:T(2,128)S(1)} collective-permute-done((s32[2,3]{1,0:T(2,128)S(1)}, s32[2,3]{1,0:T(2,128)S(1)}, u32[]{:S(2)}, u32[]{:S(2)}) %collective-permute-start.3) | collective-permute-done | bytes 56 | tf_op jit(solution)/shard_map/while/body/eval_jaxpr/ppermute | solution.py:19
  (623 shorter events, 355.5 us)
Async XLA Ops:
  1.7 150.0 %collective-permute-start.14 = (bf16[3,128,128]{2,1,0:T(8,128)(2,1)S(1)}, bf16[3,128,128]{2,1,0:T(8,128)(2,1)S(1)}, u32[]{:S(2)}, u32[]{:S(2)}) collective-permute-start(bf16[3,128,128]{2,1,0:T(8,128)(2,1)S(1)} %bitcast_select_fusion), channel_id=1, source_target_pairs={{0,992},{32,0},{64,32},{96,64},{128,96},{160,128},{192,160},{224,1... | collective-permute-start | bytes 294920 | tf_op jit(solution)/shard_map/ppermute | solution.py:19
  4.2 147.5 %collective-permute-start.4 = (bf16[3,128,128]{2,1,0:T(8,128)(2,1)S(1)}, bf16[3,128,128]{2,1,0:T(8,128)(2,1)S(1)}, u32[]{:S(2)}, u32[]{:S(2)}) collective-permute-start(bf16[3,128,128]{2,1,0:T(8,128)(2,1)S(1)} %bitcast_select_fusion), channel_id=1, source_target_pairs={{0,31},{1,0},{2,1},{3,2},{4,3},{5,4},{6,5},{7,6},{8,7},{9,8},{10,9... | collective-permute-start | bytes 294920 | tf_op jit(solution)/shard_map/ppermute | solution.py:19
  37.8 46.0 %collective-permute-start.20 = (s32[2,3]{1,0:T(2,128)S(1)}, s32[2,3]{1,0:T(2,128)S(1)}, u32[]{:S(2)}, u32[]{:S(2)}) collective-permute-start(s32[2,3]{1,0:T(2,128)S(1)} %get-tuple-element.340), channel_id=1, source_target_pairs={{0,960},{32,992},{64,0},{96,32},{128,64},{160,96},{192,128},{224,1... | collective-permute-start | bytes 80 | tf_op jit(solution)/shard_map/ppermute | solution.py:19
  43.0 42.8 %collective-permute-start.11 = (s32[2,3]{1,0:T(2,128)S(1)}, s32[2,3]{1,0:T(2,128)S(1)}, u32[]{:S(2)}, u32[]{:S(2)}) collective-permute-start(s32[2,3]{1,0:T(2,128)S(1)} %broadcast_select_fusion.16), channel_id=1, source_target_pairs={{0,28},{1,29},{2,30},{3,31},{4,0},{5,1},{6,2},{7,3},{8,4},{9,5},{1... | collective-permute-start | bytes 80 | tf_op jit(solution)/shard_map/ppermute | solution.py:19
  110.6 41.0 %collective-permute-start.13 = (s32[2,3]{1,0:T(2,128)S(1)}, s32[2,3]{1,0:T(2,128)S(1)}, u32[]{:S(2)}, u32[]{:S(2)}) collective-permute-start(s32[2,3]{1,0:T(2,128)S(1)} %broadcast_select_fusion.18), channel_id=1, source_target_pairs={{0,16},{1,17},{2,18},{3,19},{4,20},{5,21},{6,22},{7,23},{8,24},{9,... | collective-permute-start | bytes 80 | tf_op jit(solution)/shard_map/ppermute | solution.py:19
  156.3 39.6 %collective-permute-start.15 = (bf16[3,128,128]{2,1,0:T(8,128)(2,1)S(1)}, bf16[3,128,128]{2,1,0:T(8,128)(2,1)S(1)}, u32[]{:S(2)}, u32[]{:S(2)}) collective-permute-start(bf16[3,128,128]{2,1,0:T(8,128)(2,1)S(1)} %get-tuple-element.334), channel_id=1, source_target_pairs={{0,960},{32,992},{64,0},{96,32},{128,64},{160,96},{192,128},{224,1... | collective-permute-start | bytes 294920 | tf_op jit(solution)/shard_map/ppermute | solution.py:19
  158.3 39.6 %collective-permute-start.6 = (bf16[3,128,128]{2,1,0:T(8,128)(2,1)S(1)}, bf16[3,128,128]{2,1,0:T(8,128)(2,1)S(1)}, u32[]{:S(2)}, u32[]{:S(2)}) collective-permute-start(bf16[3,128,128]{2,1,0:T(8,128)(2,1)S(1)} %broadcast_select_fusion.6), channel_id=1, source_target_pairs={{0,28},{1,29},{2,30},{3,31},{4,0},{5,1},{6,2},{7,3},{8,4},{9,5},{1... | collective-permute-start | bytes 294920 | tf_op jit(solution)/shard_map/ppermute | solution.py:19
  272.0 63.8 %collective-permute-start = (bf16[3,128,128]{2,1,0:T(8,128)(2,1)S(1)}, bf16[3,128,128]{2,1,0:T(8,128)(2,1)S(1)}, u32[]{:S(2)}, u32[]{:S(2)}) collective-permute-start(bf16[3,128,128]{2,1,0:T(8,128)(2,1)S(1)} %copy.24), channel_id=1, source_target_pairs={{0,31},{1,0},{2,1},{3,2},{4,3},{5,4},{6,5},{7,6},{8,7},{9,8},{10,9... | collective-permute-start | bytes 294920 | tf_op jit(solution)/shard_map/while/body/eval_jaxpr/ppermute | solution.py:19
  369.6 44.7 %collective-permute-start = (bf16[3,128,128]{2,1,0:T(8,128)(2,1)S(1)}, bf16[3,128,128]{2,1,0:T(8,128)(2,1)S(1)}, u32[]{:S(2)}, u32[]{:S(2)}) collective-permute-start(bf16[3,128,128]{2,1,0:T(8,128)(2,1)S(1)} %copy.24), channel_id=1, source_target_pairs={{0,31},{1,0},{2,1},{3,2},{4,3},{5,4},{6,5},{7,6},{8,7},{9,8},{10,9... | collective-permute-start | bytes 294920 | tf_op jit(solution)/shard_map/while/body/eval_jaxpr/ppermute | solution.py:19
  414.3 38.0 %collective-permute-start = (bf16[3,128,128]{2,1,0:T(8,128)(2,1)S(1)}, bf16[3,128,128]{2,1,0:T(8,128)(2,1)S(1)}, u32[]{:S(2)}, u32[]{:S(2)}) collective-permute-start(bf16[3,128,128]{2,1,0:T(8,128)(2,1)S(1)} %copy.24), channel_id=1, source_target_pairs={{0,31},{1,0},{2,1},{3,2},{4,3},{5,4},{6,5},{7,6},{8,7},{9,8},{10,9... | collective-permute-start | bytes 294920 | tf_op jit(solution)/shard_map/while/body/eval_jaxpr/ppermute | solution.py:19
  452.3 36.7 %collective-permute-start = (bf16[3,128,128]{2,1,0:T(8,128)(2,1)S(1)}, bf16[3,128,128]{2,1,0:T(8,128)(2,1)S(1)}, u32[]{:S(2)}, u32[]{:S(2)}) collective-permute-start(bf16[3,128,128]{2,1,0:T(8,128)(2,1)S(1)} %copy.24), channel_id=1, source_target_pairs={{0,31},{1,0},{2,1},{3,2},{4,3},{5,4},{6,5},{7,6},{8,7},{9,8},{10,9... | collective-permute-start | bytes 294920 | tf_op jit(solution)/shard_map/while/body/eval_jaxpr/ppermute | solution.py:19
  489.0 37.3 %collective-permute-start = (bf16[3,128,128]{2,1,0:T(8,128)(2,1)S(1)}, bf16[3,128,128]{2,1,0:T(8,128)(2,1)S(1)}, u32[]{:S(2)}, u32[]{:S(2)}) collective-permute-start(bf16[3,128,128]{2,1,0:T(8,128)(2,1)S(1)} %copy.24), channel_id=1, source_target_pairs={{0,31},{1,0},{2,1},{3,2},{4,3},{5,4},{6,5},{7,6},{8,7},{9,8},{10,9... | collective-permute-start | bytes 294920 | tf_op jit(solution)/shard_map/while/body/eval_jaxpr/ppermute | solution.py:19
  526.3 36.8 %collective-permute-start = (bf16[3,128,128]{2,1,0:T(8,128)(2,1)S(1)}, bf16[3,128,128]{2,1,0:T(8,128)(2,1)S(1)}, u32[]{:S(2)}, u32[]{:S(2)}) collective-permute-start(bf16[3,128,128]{2,1,0:T(8,128)(2,1)S(1)} %copy.24), channel_id=1, source_target_pairs={{0,31},{1,0},{2,1},{3,2},{4,3},{5,4},{6,5},{7,6},{8,7},{9,8},{10,9... | collective-permute-start | bytes 294920 | tf_op jit(solution)/shard_map/while/body/eval_jaxpr/ppermute | solution.py:19
  563.1 37.3 %collective-permute-start = (bf16[3,128,128]{2,1,0:T(8,128)(2,1)S(1)}, bf16[3,128,128]{2,1,0:T(8,128)(2,1)S(1)}, u32[]{:S(2)}, u32[]{:S(2)}) collective-permute-start(bf16[3,128,128]{2,1,0:T(8,128)(2,1)S(1)} %copy.24), channel_id=1, source_target_pairs={{0,31},{1,0},{2,1},{3,2},{4,3},{5,4},{6,5},{7,6},{8,7},{9,8},{10,9... | collective-permute-start | bytes 294920 | tf_op jit(solution)/shard_map/while/body/eval_jaxpr/ppermute | solution.py:19
  635.4 35.4 %collective-permute-start = (bf16[3,128,128]{2,1,0:T(8,128)(2,1)S(1)}, bf16[3,128,128]{2,1,0:T(8,128)(2,1)S(1)}, u32[]{:S(2)}, u32[]{:S(2)}) collective-permute-start(bf16[3,128,128]{2,1,0:T(8,128)(2,1)S(1)} %copy.24), channel_id=1, source_target_pairs={{0,31},{1,0},{2,1},{3,2},{4,3},{5,4},{6,5},{7,6},{8,7},{9,8},{10,9... | collective-permute-start | bytes 294920 | tf_op jit(solution)/shard_map/while/body/eval_jaxpr/ppermute | solution.py:19
  670.9 35.7 %collective-permute-start = (bf16[3,128,128]{2,1,0:T(8,128)(2,1)S(1)}, bf16[3,128,128]{2,1,0:T(8,128)(2,1)S(1)}, u32[]{:S(2)}, u32[]{:S(2)}) collective-permute-start(bf16[3,128,128]{2,1,0:T(8,128)(2,1)S(1)} %copy.24), channel_id=1, source_target_pairs={{0,31},{1,0},{2,1},{3,2},{4,3},{5,4},{6,5},{7,6},{8,7},{9,8},{10,9... | collective-permute-start | bytes 294920 | tf_op jit(solution)/shard_map/while/body/eval_jaxpr/ppermute | solution.py:19
  706.6 72.2 %collective-permute-start = (bf16[3,128,128]{2,1,0:T(8,128)(2,1)S(1)}, bf16[3,128,128]{2,1,0:T(8,128)(2,1)S(1)}, u32[]{:S(2)}, u32[]{:S(2)}) collective-permute-start(bf16[3,128,128]{2,1,0:T(8,128)(2,1)S(1)} %copy.24), channel_id=1, source_target_pairs={{0,31},{1,0},{2,1},{3,2},{4,3},{5,4},{6,5},{7,6},{8,7},{9,8},{10,9... | collective-permute-start | bytes 294920 | tf_op jit(solution)/shard_map/while/body/eval_jaxpr/ppermute | solution.py:19
  740.1 38.6 %collective-permute-start.2 = (bf16[3,128,128]{2,1,0:T(8,128)(2,1)S(1)}, bf16[3,128,128]{2,1,0:T(8,128)(2,1)S(1)}, u32[]{:S(2)}, u32[]{:S(2)}) collective-permute-start(bf16[3,128,128]{2,1,0:T(8,128)(2,1)S(1)} %copy.26), channel_id=1, source_target_pairs={{0,992},{32,0},{64,32},{96,64},{128,96},{160,128},{192,160},{224,1... | collective-permute-start | bytes 294920 | tf_op jit(solution)/shard_map/while/body/eval_jaxpr/ppermute | solution.py:19
  742.0 36.7 %collective-permute-start.3 = (s32[2,3]{1,0:T(2,128)S(1)}, s32[2,3]{1,0:T(2,128)S(1)}, u32[]{:S(2)}, u32[]{:S(2)}) collective-permute-start(s32[2,3]{1,0:T(2,128)S(1)} %copy.27), channel_id=1, source_target_pairs={{0,992},{32,0},{64,32},{96,64},{128,96},{160,128},{192,160},{224,1... | collective-permute-start | bytes 80 | tf_op jit(solution)/shard_map/while/body/eval_jaxpr/ppermute | solution.py:19
  778.7 35.1 %collective-permute-start = (bf16[3,128,128]{2,1,0:T(8,128)(2,1)S(1)}, bf16[3,128,128]{2,1,0:T(8,128)(2,1)S(1)}, u32[]{:S(2)}, u32[]{:S(2)}) collective-permute-start(bf16[3,128,128]{2,1,0:T(8,128)(2,1)S(1)} %copy.24), channel_id=1, source_target_pairs={{0,31},{1,0},{2,1},{3,2},{4,3},{5,4},{6,5},{7,6},{8,7},{9,8},{10,9... | collective-permute-start | bytes 294920 | tf_op jit(solution)/shard_map/while/body/eval_jaxpr/ppermute | solution.py:19
  813.9 38.7 %collective-permute-start = (bf16[3,128,128]{2,1,0:T(8,128)(2,1)S(1)}, bf16[3,128,128]{2,1,0:T(8,128)(2,1)S(1)}, u32[]{:S(2)}, u32[]{:S(2)}) collective-permute-start(bf16[3,128,128]{2,1,0:T(8,128)(2,1)S(1)} %copy.24), channel_id=1, source_target_pairs={{0,31},{1,0},{2,1},{3,2},{4,3},{5,4},{6,5},{7,6},{8,7},{9,8},{10,9... | collective-permute-start | bytes 294920 | tf_op jit(solution)/shard_map/while/body/eval_jaxpr/ppermute | solution.py:19
  852.6 36.7 %collective-permute-start = (bf16[3,128,128]{2,1,0:T(8,128)(2,1)S(1)}, bf16[3,128,128]{2,1,0:T(8,128)(2,1)S(1)}, u32[]{:S(2)}, u32[]{:S(2)}) collective-permute-start(bf16[3,128,128]{2,1,0:T(8,128)(2,1)S(1)} %copy.24), channel_id=1, source_target_pairs={{0,31},{1,0},{2,1},{3,2},{4,3},{5,4},{6,5},{7,6},{8,7},{9,8},{10,9... | collective-permute-start | bytes 294920 | tf_op jit(solution)/shard_map/while/body/eval_jaxpr/ppermute | solution.py:19
  889.4 35.7 %collective-permute-start = (bf16[3,128,128]{2,1,0:T(8,128)(2,1)S(1)}, bf16[3,128,128]{2,1,0:T(8,128)(2,1)S(1)}, u32[]{:S(2)}, u32[]{:S(2)}) collective-permute-start(bf16[3,128,128]{2,1,0:T(8,128)(2,1)S(1)} %copy.24), channel_id=1, source_target_pairs={{0,31},{1,0},{2,1},{3,2},{4,3},{5,4},{6,5},{7,6},{8,7},{9,8},{10,9... | collective-permute-start | bytes 294920 | tf_op jit(solution)/shard_map/while/body/eval_jaxpr/ppermute | solution.py:19
  959.0 40.3 %collective-permute-start = (bf16[3,128,128]{2,1,0:T(8,128)(2,1)S(1)}, bf16[3,128,128]{2,1,0:T(8,128)(2,1)S(1)}, u32[]{:S(2)}, u32[]{:S(2)}) collective-permute-start(bf16[3,128,128]{2,1,0:T(8,128)(2,1)S(1)} %copy.24), channel_id=1, source_target_pairs={{0,31},{1,0},{2,1},{3,2},{4,3},{5,4},{6,5},{7,6},{8,7},{9,8},{10,9... | collective-permute-start | bytes 294920 | tf_op jit(solution)/shard_map/while/body/eval_jaxpr/ppermute | solution.py:19
  964.3 35.1 %collective-permute-start.2 = (bf16[3,128,128]{2,1,0:T(8,128)(2,1)S(1)}, bf16[3,128,128]{2,1,0:T(8,128)(2,1)S(1)}, u32[]{:S(2)}, u32[]{:S(2)}) collective-permute-start(bf16[3,128,128]{2,1,0:T(8,128)(2,1)S(1)} %copy.26), channel_id=1, source_target_pairs={{0,992},{32,0},{64,32},{96,64},{128,96},{160,128},{192,160},{224,1... | collective-permute-start | bytes 294920 | tf_op jit(solution)/shard_map/while/body/eval_jaxpr/ppermute | solution.py:19
  1033.5 42.3 %collective-permute-start = (bf16[3,128,128]{2,1,0:T(8,128)(2,1)S(1)}, bf16[3,128,128]{2,1,0:T(8,128)(2,1)S(1)}, u32[]{:S(2)}, u32[]{:S(2)}) collective-permute-start(bf16[3,128,128]{2,1,0:T(8,128)(2,1)S(1)} %copy.24), channel_id=1, source_target_pairs={{0,31},{1,0},{2,1},{3,2},{4,3},{5,4},{6,5},{7,6},{8,7},{9,8},{10,9... | collective-permute-start | bytes 294920 | tf_op jit(solution)/shard_map/while/body/eval_jaxpr/ppermute | solution.py:19
  1040.4 35.4 %collective-permute-start.2 = (bf16[3,128,128]{2,1,0:T(8,128)(2,1)S(1)}, bf16[3,128,128]{2,1,0:T(8,128)(2,1)S(1)}, u32[]{:S(2)}, u32[]{:S(2)}) collective-permute-start(bf16[3,128,128]{2,1,0:T(8,128)(2,1)S(1)} %copy.26), channel_id=1, source_target_pairs={{0,992},{32,0},{64,32},{96,64},{128,96},{160,128},{192,160},{224,1... | collective-permute-start | bytes 294920 | tf_op jit(solution)/shard_map/while/body/eval_jaxpr/ppermute | solution.py:19
  1075.8 39.9 %collective-permute-start = (bf16[3,128,128]{2,1,0:T(8,128)(2,1)S(1)}, bf16[3,128,128]{2,1,0:T(8,128)(2,1)S(1)}, u32[]{:S(2)}, u32[]{:S(2)}) collective-permute-start(bf16[3,128,128]{2,1,0:T(8,128)(2,1)S(1)} %copy.24), channel_id=1, source_target_pairs={{0,31},{1,0},{2,1},{3,2},{4,3},{5,4},{6,5},{7,6},{8,7},{9,8},{10,9... | collective-permute-start | bytes 294920 | tf_op jit(solution)/shard_map/while/body/eval_jaxpr/ppermute | solution.py:19
  1115.7 39.8 %collective-permute-start = (bf16[3,128,128]{2,1,0:T(8,128)(2,1)S(1)}, bf16[3,128,128]{2,1,0:T(8,128)(2,1)S(1)}, u32[]{:S(2)}, u32[]{:S(2)}) collective-permute-start(bf16[3,128,128]{2,1,0:T(8,128)(2,1)S(1)} %copy.24), channel_id=1, source_target_pairs={{0,31},{1,0},{2,1},{3,2},{4,3},{5,4},{6,5},{7,6},{8,7},{9,8},{10,9... | collective-permute-start | bytes 294920 | tf_op jit(solution)/shard_map/while/body/eval_jaxpr/ppermute | solution.py:19
  1120.3 35.2 %collective-permute-start.2 = (bf16[3,128,128]{2,1,0:T(8,128)(2,1)S(1)}, bf16[3,128,128]{2,1,0:T(8,128)(2,1)S(1)}, u32[]{:S(2)}, u32[]{:S(2)}) collective-permute-start(bf16[3,128,128]{2,1,0:T(8,128)(2,1)S(1)} %copy.26), channel_id=1, source_target_pairs={{0,992},{32,0},{64,32},{96,64},{128,96},{160,128},{192,160},{224,1... | collective-permute-start | bytes 294920 | tf_op jit(solution)/shard_map/while/body/eval_jaxpr/ppermute | solution.py:19
  1155.5 40.5 %collective-permute-start = (bf16[3,128,128]{2,1,0:T(8,128)(2,1)S(1)}, bf16[3,128,128]{2,1,0:T(8,128)(2,1)S(1)}, u32[]{:S(2)}, u32[]{:S(2)}) collective-permute-start(bf16[3,128,128]{2,1,0:T(8,128)(2,1)S(1)} %copy.24), channel_id=1, source_target_pairs={{0,31},{1,0},{2,1},{3,2},{4,3},{5,4},{6,5},{7,6},{8,7},{9,8},{10,9... | collective-permute-start | bytes 294920 | tf_op jit(solution)/shard_map/while/body/eval_jaxpr/ppermute | solution.py:19
  1160.1 35.9 %collective-permute-start.2 = (bf16[3,128,128]{2,1,0:T(8,128)(2,1)S(1)}, bf16[3,128,128]{2,1,0:T(8,128)(2,1)S(1)}, u32[]{:S(2)}, u32[]{:S(2)}) collective-permute-start(bf16[3,128,128]{2,1,0:T(8,128)(2,1)S(1)} %copy.26), channel_id=1, source_target_pairs={{0,992},{32,0},{64,32},{96,64},{128,96},{160,128},{192,160},{224,1... | collective-permute-start | bytes 294920 | tf_op jit(solution)/shard_map/while/body/eval_jaxpr/ppermute | solution.py:19
  1196.0 42.8 %collective-permute-start = (bf16[3,128,128]{2,1,0:T(8,128)(2,1)S(1)}, bf16[3,128,128]{2,1,0:T(8,128)(2,1)S(1)}, u32[]{:S(2)}, u32[]{:S(2)}) collective-permute-start(bf16[3,128,128]{2,1,0:T(8,128)(2,1)S(1)} %copy.24), channel_id=1, source_target_pairs={{0,31},{1,0},{2,1},{3,2},{4,3},{5,4},{6,5},{7,6},{8,7},{9,8},{10,9... | collective-permute-start | bytes 294920 | tf_op jit(solution)/shard_map/while/body/eval_jaxpr/ppermute | solution.py:19
  1200.6 38.2 %collective-permute-start.2 = (bf16[3,128,128]{2,1,0:T(8,128)(2,1)S(1)}, bf16[3,128,128]{2,1,0:T(8,128)(2,1)S(1)}, u32[]{:S(2)}, u32[]{:S(2)}) collective-permute-start(bf16[3,128,128]{2,1,0:T(8,128)(2,1)S(1)} %copy.26), channel_id=1, source_target_pairs={{0,992},{32,0},{64,32},{96,64},{128,96},{160,128},{192,160},{224,1... | collective-permute-start | bytes 294920 | tf_op jit(solution)/shard_map/while/body/eval_jaxpr/ppermute | solution.py:19
  1202.5 36.3 %collective-permute-start.3 = (s32[2,3]{1,0:T(2,128)S(1)}, s32[2,3]{1,0:T(2,128)S(1)}, u32[]{:S(2)}, u32[]{:S(2)}) collective-permute-start(s32[2,3]{1,0:T(2,128)S(1)} %copy.27), channel_id=1, source_target_pairs={{0,992},{32,0},{64,32},{96,64},{128,96},{160,128},{192,160},{224,1... | collective-permute-start | bytes 80 | tf_op jit(solution)/shard_map/while/body/eval_jaxpr/ppermute | solution.py:19
  1238.8 41.1 %collective-permute-start = (bf16[3,128,128]{2,1,0:T(8,128)(2,1)S(1)}, bf16[3,128,128]{2,1,0:T(8,128)(2,1)S(1)}, u32[]{:S(2)}, u32[]{:S(2)}) collective-permute-start(bf16[3,128,128]{2,1,0:T(8,128)(2,1)S(1)} %copy.24), channel_id=1, source_target_pairs={{0,31},{1,0},{2,1},{3,2},{4,3},{5,4},{6,5},{7,6},{8,7},{9,8},{10,9... | collective-permute-start | bytes 294920 | tf_op jit(solution)/shard_map/while/body/eval_jaxpr/ppermute | solution.py:19
  1243.4 36.5 %collective-permute-start.2 = (bf16[3,128,128]{2,1,0:T(8,128)(2,1)S(1)}, bf16[3,128,128]{2,1,0:T(8,128)(2,1)S(1)}, u32[]{:S(2)}, u32[]{:S(2)}) collective-permute-start(bf16[3,128,128]{2,1,0:T(8,128)(2,1)S(1)} %copy.26), channel_id=1, source_target_pairs={{0,992},{32,0},{64,32},{96,64},{128,96},{160,128},{192,160},{224,1... | collective-permute-start | bytes 294920 | tf_op jit(solution)/shard_map/while/body/eval_jaxpr/ppermute | solution.py:19
  1279.9 42.4 %collective-permute-start = (bf16[3,128,128]{2,1,0:T(8,128)(2,1)S(1)}, bf16[3,128,128]{2,1,0:T(8,128)(2,1)S(1)}, u32[]{:S(2)}, u32[]{:S(2)}) collective-permute-start(bf16[3,128,128]{2,1,0:T(8,128)(2,1)S(1)} %copy.24), channel_id=1, source_target_pairs={{0,31},{1,0},{2,1},{3,2},{4,3},{5,4},{6,5},{7,6},{8,7},{9,8},{10,9... | collective-permute-start | bytes 294920 | tf_op jit(solution)/shard_map/while/body/eval_jaxpr/ppermute | solution.py:19
  1284.5 37.8 %collective-permute-start.2 = (bf16[3,128,128]{2,1,0:T(8,128)(2,1)S(1)}, bf16[3,128,128]{2,1,0:T(8,128)(2,1)S(1)}, u32[]{:S(2)}, u32[]{:S(2)}) collective-permute-start(bf16[3,128,128]{2,1,0:T(8,128)(2,1)S(1)} %copy.26), channel_id=1, source_target_pairs={{0,992},{32,0},{64,32},{96,64},{128,96},{160,128},{192,160},{224,1... | collective-permute-start | bytes 294920 | tf_op jit(solution)/shard_map/while/body/eval_jaxpr/ppermute | solution.py:19
  1286.4 35.8 %collective-permute-start.3 = (s32[2,3]{1,0:T(2,128)S(1)}, s32[2,3]{1,0:T(2,128)S(1)}, u32[]{:S(2)}, u32[]{:S(2)}) collective-permute-start(s32[2,3]{1,0:T(2,128)S(1)} %copy.27), channel_id=1, source_target_pairs={{0,992},{32,0},{64,32},{96,64},{128,96},{160,128},{192,160},{224,1... | collective-permute-start | bytes 80 | tf_op jit(solution)/shard_map/while/body/eval_jaxpr/ppermute | solution.py:19
  1322.3 37.5 %collective-permute-start = (bf16[3,128,128]{2,1,0:T(8,128)(2,1)S(1)}, bf16[3,128,128]{2,1,0:T(8,128)(2,1)S(1)}, u32[]{:S(2)}, u32[]{:S(2)}) collective-permute-start(bf16[3,128,128]{2,1,0:T(8,128)(2,1)S(1)} %copy.24), channel_id=1, source_target_pairs={{0,31},{1,0},{2,1},{3,2},{4,3},{5,4},{6,5},{7,6},{8,7},{9,8},{10,9... | collective-permute-start | bytes 294920 | tf_op jit(solution)/shard_map/while/body/eval_jaxpr/ppermute | solution.py:19
  1359.8 44.1 %collective-permute-start = (bf16[3,128,128]{2,1,0:T(8,128)(2,1)S(1)}, bf16[3,128,128]{2,1,0:T(8,128)(2,1)S(1)}, u32[]{:S(2)}, u32[]{:S(2)}) collective-permute-start(bf16[3,128,128]{2,1,0:T(8,128)(2,1)S(1)} %copy.24), channel_id=1, source_target_pairs={{0,31},{1,0},{2,1},{3,2},{4,3},{5,4},{6,5},{7,6},{8,7},{9,8},{10,9... | collective-permute-start | bytes 294920 | tf_op jit(solution)/shard_map/while/body/eval_jaxpr/ppermute | solution.py:19
  1364.4 39.5 %collective-permute-start.2 = (bf16[3,128,128]{2,1,0:T(8,128)(2,1)S(1)}, bf16[3,128,128]{2,1,0:T(8,128)(2,1)S(1)}, u32[]{:S(2)}, u32[]{:S(2)}) collective-permute-start(bf16[3,128,128]{2,1,0:T(8,128)(2,1)S(1)} %copy.26), channel_id=1, source_target_pairs={{0,992},{32,0},{64,32},{96,64},{128,96},{160,128},{192,160},{224,1... | collective-permute-start | bytes 294920 | tf_op jit(solution)/shard_map/while/body/eval_jaxpr/ppermute | solution.py:19
  1366.3 37.6 %collective-permute-start.3 = (s32[2,3]{1,0:T(2,128)S(1)}, s32[2,3]{1,0:T(2,128)S(1)}, u32[]{:S(2)}, u32[]{:S(2)}) collective-permute-start(s32[2,3]{1,0:T(2,128)S(1)} %copy.27), channel_id=1, source_target_pairs={{0,992},{32,0},{64,32},{96,64},{128,96},{160,128},{192,160},{224,1... | collective-permute-start | bytes 80 | tf_op jit(solution)/shard_map/while/body/eval_jaxpr/ppermute | solution.py:19
  1403.9 40.1 %collective-permute-start = (bf16[3,128,128]{2,1,0:T(8,128)(2,1)S(1)}, bf16[3,128,128]{2,1,0:T(8,128)(2,1)S(1)}, u32[]{:S(2)}, u32[]{:S(2)}) collective-permute-start(bf16[3,128,128]{2,1,0:T(8,128)(2,1)S(1)} %copy.24), channel_id=1, source_target_pairs={{0,31},{1,0},{2,1},{3,2},{4,3},{5,4},{6,5},{7,6},{8,7},{9,8},{10,9... | collective-permute-start | bytes 294920 | tf_op jit(solution)/shard_map/while/body/eval_jaxpr/ppermute | solution.py:19
  1408.5 35.5 %collective-permute-start.2 = (bf16[3,128,128]{2,1,0:T(8,128)(2,1)S(1)}, bf16[3,128,128]{2,1,0:T(8,128)(2,1)S(1)}, u32[]{:S(2)}, u32[]{:S(2)}) collective-permute-start(bf16[3,128,128]{2,1,0:T(8,128)(2,1)S(1)} %copy.26), channel_id=1, source_target_pairs={{0,992},{32,0},{64,32},{96,64},{128,96},{160,128},{192,160},{224,1... | collective-permute-start | bytes 294920 | tf_op jit(solution)/shard_map/while/body/eval_jaxpr/ppermute | solution.py:19
  1444.0 36.8 %collective-permute-start = (bf16[3,128,128]{2,1,0:T(8,128)(2,1)S(1)}, bf16[3,128,128]{2,1,0:T(8,128)(2,1)S(1)}, u32[]{:S(2)}, u32[]{:S(2)}) collective-permute-start(bf16[3,128,128]{2,1,0:T(8,128)(2,1)S(1)} %copy.24), channel_id=1, source_target_pairs={{0,31},{1,0},{2,1},{3,2},{4,3},{5,4},{6,5},{7,6},{8,7},{9,8},{10,9... | collective-permute-start | bytes 294920 | tf_op jit(solution)/shard_map/while/body/eval_jaxpr/ppermute | solution.py:19
  1480.8 38.7 %collective-permute-start = (bf16[3,128,128]{2,1,0:T(8,128)(2,1)S(1)}, bf16[3,128,128]{2,1,0:T(8,128)(2,1)S(1)}, u32[]{:S(2)}, u32[]{:S(2)}) collective-permute-start(bf16[3,128,128]{2,1,0:T(8,128)(2,1)S(1)} %copy.24), channel_id=1, source_target_pairs={{0,31},{1,0},{2,1},{3,2},{4,3},{5,4},{6,5},{7,6},{8,7},{9,8},{10,9... | collective-permute-start | bytes 294920 | tf_op jit(solution)/shard_map/while/body/eval_jaxpr/ppermute | solution.py:19
  (101 other events, 2372.5 us)
where the time goes:
time: 1530 us; the launch traced here: 1520 us
  waiting for transfers between devices  997 us (65%)
  starting transfers between devices  459 us (30%)
  matrix products  40.8 us (3%)
    ppermute x144, waiting for transfers between devices, passed_along(): lax.ppermute(value, axis, [(i, (i + by) % size) for i in range(size)])  997 us
    ppermute x144, starting transfers between devices, passed_along(): lax.ppermute(value, axis, [(i, (i + by) % size) for i in range(size)])  459 us
    dot_general x32, matrix products, contribute(): jnp.einsum('oab,abij->oij', weights, products, precision=lax.Precision.HI...  32.1 us
  transfers between devices with their start and end apart: 144, of which 39 were waited for; matrix products, arithmetic and copies ran while one was open for 4% of the time, Pallas kernels for 0%

commit v1 on v0

v1 whole, which is shorter than its diff:
```python
import functools

import jax
import jax.numpy as jnp
from jax import lax
from jax.experimental import pallas as pl
from jax.experimental.pallas import tpu as pltpu
from jax.sharding import PartitionSpec as P

MESH = pl.DeviceIdType.MESH
BLOCK = 128
SLOTS = 3
KEPT = 6
META = SLOTS * BLOCK
TILE = META + 16
HALF = 208
HALVES = ((0, HALF), (HALF, TILE - HALF))
RUN = 16
NONE = 255


def device(z_hi, x, y, k, core):
    return (z_hi * 16 + x * 4 + y, k * 2 + core)


def turn(value, by):
    return lax.rem(value + by, 4)


def flag(condition):
    return jnp.where(condition, 1, 0)


def gather_kernel(
    p_rows, p_cols, p_count, blocks, row_tiles, col_tiles,
    meta, row_recv, col_recv, anti_recv, own_sem, send_own, send_row, send_pair, send_xy,
    ready_pair, ready_jump, ready_anti,
):
    row, col = lax.axis_index("row"), lax.axis_index("col")
    z_hi, x, y = row // 16, (row // 4) % 4, row % 4
    k, core = col // 2, col % 2
    here = functools.partial(device, z_hi, x, y)
    in_plane = lambda nx, ny: device(z_hi, nx, ny, k, core)
    pair = here(k, 1 - core)
    antipode = device(1 - z_hi, x, y, k, core)

    def signal(semaphore, target):
        pl.semaphore_signal(semaphore, inc=1, device_id=target, device_id_type=MESH)

    first_plane = (z_hi == 0) & (k == 0)
    is_late = first_plane & (x == 0) & (y == 0) & (core == 0)
    late_pair = first_plane & (x == 0) & (y == 0) & (core == 1)
    late_plane = first_plane & (core == 0) & ((x == 0) != (y == 0))

    copies = []

    def local(src, dst, number):
        copy = pltpu.make_async_copy(src, dst, own_sem.at[number])
        copy.start()
        copies.append(copy)

    mine_row, mine_col = row_tiles.at[col], col_tiles.at[row]
    local(blocks, mine_row.at[pl.ds(0, META)], 0)
    local(blocks, mine_col.at[pl.ds(0, META)], 1)

    barrier = pltpu.get_barrier_semaphore()

    @pl.when((core == 0) & (k > 0))
    def _():
        for other in range(2):
            signal(barrier, here(k - 1, other))

    @pl.when((core == 1) & (k < RUN - 1))
    def _():
        for other in range(2):
            signal(barrier, here(k + 1, other))

    @pl.when(jnp.logical_not(is_late))
    def _():
        signal(barrier, pair)
        for d in range(1, 4):
            signal(barrier, in_plane(turn(x, d), y))
            signal(barrier, in_plane(x, turn(y, d)))

    @pl.when(z_hi == 0)
    def _():
        signal(barrier, antipode)

    @pl.when((core == 1) & (k == 3))
    def _():
        for source in range(8, 16):
            for other in range(2):
                signal(barrier, here(source, other))

    @pl.when((core == 1) & (k == 7))
    def _():
        for source in range(12, 16):
            for other in range(2):
                signal(barrier, here(source, other))

    @pl.when(k < 8)
    def _():
        signal(barrier, here(12, 0))

    @pl.when(k < 4)
    def _():
        signal(barrier, here(8, 0))

    lane = lax.broadcasted_iota(jnp.int32, (16, BLOCK), 1)
    codes = jnp.zeros((16, BLOCK), jnp.int32)
    for slot in range(SLOTS):
        code = jnp.where(slot < p_count[0], p_rows[slot] * 16 + p_cols[slot], NONE)
        codes = jnp.where(lane == slot, code, codes)
    meta[...] = codes.astype(jnp.float32).astype(jnp.bfloat16)
    local(meta, mine_row.at[pl.ds(META, 16)], 2)
    local(meta, mine_col.at[pl.ds(META, 16)], 3)

    expected = (
        flag(k < RUN - 1) + flag(k > 0) + 1 - flag(late_pair) + 6 - flag(late_plane) + flag(k >= 8) + flag(k >= 12)
        + 8 * flag((core == 0) & (k == 8)) + 16 * flag((core == 0) & (k == 12)) + z_hi
    )
    pl.semaphore_wait(barrier, expected)

    @pl.when(z_hi == 1)
    def _():
        signal(ready_anti, antipode)

    @pl.when(is_late)
    def _():
        signal(ready_pair, pair)
        for d in range(1, 4):
            signal(ready_pair, in_plane(turn(x, d), y))
            signal(ready_pair, in_plane(x, turn(y, d)))

    @pl.when((core == 0) & (k == 8))
    def _():
        for source in range(0, 4):
            for other in range(2):
                signal(ready_jump, here(source, other))

    @pl.when((core == 0) & (k == 12))
    def _():
        for source in range(0, 8):
            for other in range(2):
                signal(ready_jump, here(source, other))

    for copy in copies:
        copy.wait()

    def send(src, dst, send_sem, recv_sem, target):
        return pltpu.make_async_remote_copy(
            src_ref=src, dst_ref=dst, send_sem=send_sem, recv_sem=recv_sem, device_id=target, device_id_type=MESH
        )

    def row_send(tile, send_sem, target):
        return send(row_tiles.at[tile], row_tiles.at[tile], send_sem, row_recv.at[tile], target)

    anti_send = send(mine_col, mine_col, send_own.at[0], anti_recv, antipode)
    left_send = row_send(col, send_own.at[1], here(k - 1, 1))
    right_send = row_send(col, send_own.at[2], here(k + 1, 0))
    pair_send = row_send(col, send_own.at[3], pair)
    jumps = (
        (k >= 12, row_send(col, send_own.at[4], here(7, 1))),
        (k >= 8, row_send(col, send_own.at[5], here(3, 1))),
        (k < 4, row_send(col, send_own.at[4], here(8, 0))),
        (k < 8, row_send(col, send_own.at[5], here(12, 0))),
    )

    @pl.when(z_hi == 1)
    def _():
        anti_send.start()

    for wanted, jump in jumps[:2]:
        pl.when(wanted)(jump.start)
    pl.when(k > 0)(left_send.start)
    pl.when(k < RUN - 1)(right_send.start)

    def half_send(side, tile, half, number, target):
        low, size = HALVES[half]
        part = col_tiles.at[tile, pl.ds(low, size)]
        return send(part, part, send_xy.at[side, number], col_recv.at[tile, half], target)

    def plane_tile(side, nx, ny):
        z = z_hi if side == 0 else 1 - z_hi
        return z * 16 + nx * 4 + ny

    def plane_own(side):
        mine = plane_tile(side, x, y)
        return [
            half_send(side, mine, half, number * 6 + (d - 1) * 2 + half, in_plane(turn(x, d), y) if along_x else in_plane(x, turn(y, d)))
            for number in range(2)
            for d in (2, 1, 3)
            for half in range(2)
            for along_x in ((half == 0) == (number == 0),)
        ]

    def plane_forward(side, d):
        from_x = plane_tile(side, turn(x, 4 - d), y)
        from_y = plane_tile(side, x, turn(y, 4 - d))
        first = [half_send(side, from_x, 0, 12 + (d - 1) * 6 + e - 1, in_plane(x, turn(y, e))) for e in (2, 1, 3)]
        second = [half_send(side, from_y, 1, 15 + (d - 1) * 6 + e - 1, in_plane(turn(x, e), y)) for e in (2, 1, 3)]
        return first, second

    def arrived(side, tile, half):
        half_send(side, tile, half, 0, pair).wait_recv()

    def plane_first(side):
        for copy in plane_own(side):
            copy.start()

    def plane_second(side):
        for d in (1, 3, 2):
            first, second = plane_forward(side, d)
            arrived(side, plane_tile(side, turn(x, 4 - d), y), 0)
            for copy in first:
                copy.start()
            arrived(side, plane_tile(side, x, turn(y, 4 - d)), 1)
            for copy in second:
                copy.start()

    def plane_rest(side):
        for d in range(1, 4):
            arrived(side, plane_tile(side, turn(x, d), y), 1)
            arrived(side, plane_tile(side, x, turn(y, d)), 0)
            for e in range(1, 4):
                for half in range(2):
                    arrived(side, plane_tile(side, turn(x, d), turn(y, e)), half)
        for copy in plane_own(side):
            copy.wait_send()
        for d in range(1, 4):
            for copies_of in plane_forward(side, d):
                for copy in copies_of:
                    copy.wait_send()

    @pl.when(late_plane)
    def _():
        pl.semaphore_wait(ready_pair, 1)

    plane_first(0)

    @pl.when(late_pair)
    def _():
        pl.semaphore_wait(ready_pair, 1)

    pair_send.start()
    plane_second(0)

    step = 2 * core - 1
    onward = here(jnp.clip(k - step, 0, RUN - 1), core)

    def is_valid(source):
        return (source >= 0) & (source < RUN)

    def goes_on(source):
        right = (k < RUN - 1) & jnp.logical_not((k == 7) & (source < 4)) & jnp.logical_not((k == 11) & (source < 8))
        left = (k > 0) & jnp.logical_not((k == 8) & (source >= 12)) & jnp.logical_not((k == 4) & (source >= 8))
        return jnp.where(core == 0, flag(right), flag(left)) == 1

    jump_at = 4
    anti_at = jnp.where((core == 1) & (z_hi == 0), jnp.where(k == 0, 8, 12), RUN)
    anti_next = RUN

    def anti_first():
        @pl.when(z_hi == 0)
        def _():
            pl.semaphore_wait(ready_anti, 1)
            anti_send.start()

        anti_send.wait_recv()
        plane_first(1)

    def jump_right():
        pl.semaphore_wait(ready_jump, flag(k < 8) + flag(k < 4))
        for wanted, jump in jumps[2:]:
            pl.when(wanted)(jump.start)

    def stream(t, carry):
        source = k + step * t

        @pl.when(is_valid(source))
        def _():
            for other in range(2):
                tile = source * 2 + other
                row_send(tile, send_row.at[tile], pair).wait_recv()
                pl.when(goes_on(source))(row_send(tile, send_row.at[tile], onward).start)
                row_send(tile, send_pair.at[tile], pair).start()

        @pl.when((t == jump_at) & (k < 8))
        def _():
            jump_right()

        @pl.when(t == anti_at)
        def _():
            anti_first()

        return carry

    lax.fori_loop(1, RUN, stream, 0)

    @pl.when(anti_at == RUN)
    def _():
        anti_first()

    plane_second(1)

    row_send(k * 2 + 1 - core, send_own.at[3], pair).wait_recv()

    def settle(t, carry):
        source, opposite = k + step * t, k - step * t

        @pl.when(is_valid(opposite))
        def _():
            for other in range(2):
                row_send(opposite * 2 + other, send_pair.at[0], pair).wait_recv()

        @pl.when(is_valid(source))
        def _():
            for other in range(2):
                tile = source * 2 + other
                pl.when(goes_on(source))(row_send(tile, send_row.at[tile], onward).wait_send)
                row_send(tile, send_pair.at[tile], pair).wait_send()

        return carry

    lax.fori_loop(1, RUN, settle, 0)
    plane_rest(0)
    plane_rest(1)
    anti_send.wait_send()
    pair_send.wait_send()
    pl.when(k > 0)(left_send.wait_send)
    pl.when(k < RUN - 1)(right_send.wait_send)
    for wanted, jump in jumps:
        pl.when(wanted)(jump.wait_send)


DEPTH = 8


def multiply_kernel(kept_rows, kept_cols, row_tiles, col_tiles, out, meta, codes, index, found, left, right, meta_sem, index_sem, sems):
    tiles = row_tiles.shape[0]
    loads = [
        pltpu.make_async_copy(tiles_of.at[:, pl.ds(META, 16), :], meta.at[side], meta_sem.at[side])
        for side, tiles_of in enumerate((row_tiles, col_tiles))
    ]
    for load in loads:
        load.start()
    for load in loads:
        load.wait()
    for side in range(2):
        codes[pl.ds(side * tiles, tiles), :] = meta[side].astype(jnp.float32)[:, 0, :].astype(jnp.int32)
    to_index = pltpu.make_async_copy(codes, index, index_sem)
    to_index.start()
    out[...] = jnp.zeros(out.shape, out.dtype)
    kept = [kept_rows[o] * 16 + kept_cols[o] for o in range(KEPT)]
    to_index.wait()

    def fetch(number):
        entry = found[number]
        a, b = entry // 4096, (entry // 8) % 512
        slot = number % DEPTH
        return (
            pltpu.make_async_copy(row_tiles.at[a // 4, pl.ds((a % 4) * BLOCK, BLOCK)], left.at[slot], sems.at[0, slot]),
            pltpu.make_async_copy(col_tiles.at[b // 4, pl.ds((b % 4) * BLOCK, BLOCK)], right.at[slot], sems.at[1, slot]),
        )

    def start(number):
        for copy in fetch(number):
            copy.start()

    def search(inner, count):
        lefts = [index[inner, s] for s in range(SLOTS)]
        rights = [index[inner + tiles, s] for s in range(SLOTS)]
        hits = [
            [flag((lefts[a] != NONE) & ((lefts[a] & 15) == (rights[b] >> 4))) for b in range(SLOTS)] for a in range(SLOTS)
        ]

        def collect(count):
            for a in range(SLOTS):
                for b in range(SLOTS):
                    wanted = (lefts[a] & 240) | (rights[b] & 15)

                    def record(count, a=a, b=b, wanted=wanted):
                        for o in range(KEPT):
                            is_kept = kept[o] == wanted

                            @pl.when(is_kept)
                            def _(count=count, o=o):
                                found[count] = (inner * 4 + a) * 4096 + (inner * 4 + b) * 8 + o

                                @pl.when(count < DEPTH)
                                def _():
                                    start(count)

                            count = count + flag(is_kept)
                        return count

                    count = lax.cond(hits[a][b] == 1, record, lambda count: count, count)
            return count

        any_hit = sum(hits[a][b] for a in range(SLOTS) for b in range(SLOTS))
        return lax.cond(any_hit > 0, collect, lambda count: count, count)

    total = lax.fori_loop(0, tiles, search, 0)

    def work(number, carry):
        slot = number % DEPTH
        for copy in fetch(number):
            copy.wait()
        o = found[number] % 8
        out[o] += jnp.dot(left[slot], right[slot], preferred_element_type=jnp.float32)

        @pl.when(number + DEPTH < total)
        def _():
            start(number + DEPTH)

        return carry

    lax.fori_loop(0, total, work, 0)


def body(p_blocks, p_rows, p_cols, p_count, kept_rows, kept_cols):
    tiles = 32
    anywhere = pl.BlockSpec(memory_space=pl.ANY)
    scalars = pl.BlockSpec(memory_space=pltpu.SMEM)
    tile_list = jax.ShapeDtypeStruct((tiles, TILE, BLOCK), jnp.bfloat16)
    row_tiles, col_tiles = pl.pallas_call(
        gather_kernel,
        out_shape=(tile_list, tile_list),
        in_specs=[scalars, scalars, scalars, anywhere],
        out_specs=(anywhere, anywhere),
        scratch_shapes=[
            pltpu.VMEM((16, BLOCK), jnp.bfloat16),
            pltpu.SemaphoreType.DMA((tiles,)),
            pltpu.SemaphoreType.DMA((tiles, 2)),
            pltpu.SemaphoreType.DMA,
            pltpu.SemaphoreType.DMA((4,)),
            pltpu.SemaphoreType.DMA((6,)),
            pltpu.SemaphoreType.DMA((tiles,)),
            pltpu.SemaphoreType.DMA((tiles,)),
            pltpu.SemaphoreType.DMA((2, 30)),
            pltpu.SemaphoreType.REGULAR,
            pltpu.SemaphoreType.REGULAR,
            pltpu.SemaphoreType.REGULAR,
        ],
        compiler_params=pltpu.CompilerParams(collective_id=0, has_side_effects=True),
        name="gather_tiles",
    )(p_rows.reshape(SLOTS), p_cols.reshape(SLOTS), p_count.reshape(1), p_blocks.reshape(META, BLOCK))
    result = pl.pallas_call(
        multiply_kernel,
        out_shape=jax.ShapeDtypeStruct((KEPT, BLOCK, BLOCK), jnp.float32),
        in_specs=[scalars, scalars, anywhere, anywhere],
        out_specs=pl.BlockSpec(memory_space=pltpu.VMEM),
        scratch_shapes=[
            pltpu.VMEM((2, tiles, 16, BLOCK), jnp.bfloat16),
            pltpu.VMEM((2 * tiles, BLOCK), jnp.int32),
            pltpu.SMEM((2 * tiles, BLOCK), jnp.int32),
            pltpu.SMEM((tiles * SLOTS * KEPT,), jnp.int32),
            pltpu.VMEM((DEPTH, BLOCK, BLOCK), jnp.bfloat16),
            pltpu.VMEM((DEPTH, BLOCK, BLOCK), jnp.bfloat16),
            pltpu.SemaphoreType.DMA((2,)),
            pltpu.SemaphoreType.DMA,
            pltpu.SemaphoreType.DMA((2, DEPTH)),
        ],
        compiler_params=pltpu.CompilerParams(vmem_limit_bytes=16 * 2**20),
        name="multiply_pairs",
    )(kept_rows.reshape(KEPT), kept_cols.reshape(KEPT), row_tiles, col_tiles)
    return result[None, None]


def solution(mesh):
    placed = (
        P("row", "col", None, None, None),
        P("row", "col", None),
        P("row", "col", None),
        P("row", "col"),
        P("row", "col", None),
        P("row", "col", None),
    )
    return jax.shard_map(
        body,
        mesh=mesh,
        in_specs=placed,
        out_specs=P("row", "col", None, None, None),
        check_vma=False,
    )
```

time: 1530 us -> 139 us (0.09)
  the two profiles are of different devices: /device:TPU:63 before, /device:TPU:992 now
where the time goes in v1:
time: 139 us
  Pallas kernels  133 us (96%)
  local copies, waits for them, and re-layouts  5.15 us (4%)
    pallas_call x1, Pallas kernels, body(): pl.pallas_call(gather_kernel, out_shape=(tile_list, tile_list), in_specs=...  126 us
    pallas_call x1, Pallas kernels, body(): pl.pallas_call(multiply_kernel, out_shape=jax.ShapeDtypeStruct((KEPT, BLO...  7.04 us
    unnamed x8, local copies, waits for them, and re-layouts  5.15 us

profile of v1, /device:TPU:992, one launch (start us, length us, event | category | flops | bytes accessed | tf_op | source)
XLA Modules:
  0.0 138.7 jit_solution(17034810405616255582)
XLA Ops:
  0.7 125.8 %gather_tiles.1 = (bf16[32,400,128]{2,1,0:T(8,128)(2,1)}, bf16[32,400,128]{2,1,0:T(8,128)(2,1)}) custom-call(s32[3]{0:T(128)} %bitcast.11, s32[3]{0:T(128)} %bitcast.12, s32[1]{0:T(128)} %bitcast.7.p_count, bf16[384,128]{1,0:T(8,128)(2,1)} %bitcast.10), custom_call_target="tpu_custom_call" | custom-call | tf_op jit(solution)/shard_map/gather_tiles/pallas_call | solution.py:426
  126.5 0.0 copy-start
  126.5 1.9 %copy-done = bf16[32,400,128]{2,1,0:T(8,128)(2,1)S(1)} copy-done((bf16[32,400,128]{2,1,0:T(8,128)(2,1)S(1)}, bf16[32,400,128]{2,1,0:T(8,128)(2,1)}, u32[]{:S(2)}) %copy-start) | copy-done | bytes 3276824
  128.4 0.0 copy-start.1
  128.4 1.9 %copy-done.1 = bf16[32,400,128]{2,1,0:T(8,128)(2,1)S(1)} copy-done((bf16[32,400,128]{2,1,0:T(8,128)(2,1)S(1)}, bf16[32,400,128]{2,1,0:T(8,128)(2,1)}, u32[]{:S(2)}) %copy-start.1) | copy-done | bytes 3276824
  130.3 0.0 copy-start.2
  130.3 0.7 copy-done.2
  131.0 0.0 copy-start.3
  131.0 0.7 copy-done.3
  131.6 7.0 %multiply_pairs.1 = f32[6,128,128]{2,1,0:T(8,128)} custom-call(s32[6]{0:T(128)S(1)} %bitcast.8, s32[6]{0:T(128)S(1)} %bitcast.9, bf16[32,400,128]{2,1,0:T(8,128)(2,1)S(1)} %copy-done, bf16[32,400,128]{2,1,0:T(8,128)(2,1)S(1)} %copy-done.1), custom_call_target="tpu_custom_call" | custom-call | tf_op jit(solution)/shard_map/multiply_pairs/pallas_call | solution.py:448
Async XLA Ops:
  126.5 1.9 %copy-start = (bf16[32,400,128]{2,1,0:T(8,128)(2,1)S(1)}, bf16[32,400,128]{2,1,0:T(8,128)(2,1)}, u32[]{:S(2)}) copy-start(bf16[32,400,128]{2,1,0:T(8,128)(2,1)} %get-tuple-element.7.row_tiles) | copy-start | bytes 9830404
  128.4 1.9 %copy-start.1 = (bf16[32,400,128]{2,1,0:T(8,128)(2,1)S(1)}, bf16[32,400,128]{2,1,0:T(8,128)(2,1)}, u32[]{:S(2)}) copy-start(bf16[32,400,128]{2,1,0:T(8,128)(2,1)} %get-tuple-element.8.col_tiles) | copy-start | bytes 9830404
  130.3 0.7 copy-start.2
  131.0 0.7 copy-start.3

commit v2 on v1

v2 whole, which is shorter than its diff:
```python
import functools

import jax
import jax.numpy as jnp
from jax import lax
from jax.experimental import pallas as pl
from jax.experimental.pallas import tpu as pltpu
from jax.sharding import PartitionSpec as P

MESH = pl.DeviceIdType.MESH
BLOCK = 128
SLOTS = 3
KEPT = 6
META = SLOTS * BLOCK
TILE = META + 16
HALF = 208
HALVES = ((0, HALF), (HALF, TILE - HALF))
PIECES = ((0, 128), (128, 128), (256, TILE - 256))
RUN = 16
NO_ROW, NO_COL = 20, 30


def device(z_hi, x, y, k, core):
    return (z_hi * 16 + x * 4 + y, k * 2 + core)


def turn(value, by):
    return lax.rem(value + by, 4)


def flag(condition):
    return jnp.where(condition, 1, 0)


def square_kernel(
    p_rows, p_cols, p_count, kept_rows, kept_cols, blocks, out,
    row_tiles, col_tiles, chosen, meta, row_recv, col_recv, anti_recv, own_sem, send_own, send_row, send_pair, send_xy,
    ready_pair, ready_anti,
):
    row, col = lax.axis_index("row"), lax.axis_index("col")
    z_hi, x, y = row // 16, (row // 4) % 4, row % 4
    k, core = col // 2, col % 2
    here = functools.partial(device, z_hi, x, y)
    in_plane = lambda nx, ny: device(z_hi, nx, ny, k, core)
    pair = here(k, 1 - core)
    antipode = device(1 - z_hi, x, y, k, core)

    def signal(semaphore, target):
        pl.semaphore_signal(semaphore, inc=1, device_id=target, device_id_type=MESH)

    first_plane = (z_hi == 0) & (k == 0)
    is_late = first_plane & (x == 0) & (y == 0) & (core == 0)
    late_pair = first_plane & (x == 0) & (y == 0) & (core == 1)
    late_plane = first_plane & (core == 0) & ((x == 0) != (y == 0))

    copies = []

    def local(src, dst, number):
        copy = pltpu.make_async_copy(src, dst, own_sem.at[number])
        copy.start()
        copies.append(copy)

    mine_row, mine_col = row_tiles.at[col], col_tiles.at[row]
    local(blocks, mine_row.at[pl.ds(0, META)], 0)
    local(blocks, mine_col.at[pl.ds(0, META)], 1)

    barrier = pltpu.get_barrier_semaphore()

    @pl.when((core == 0) & (k > 0))
    def _():
        for other in range(2):
            signal(barrier, here(k - 1, other))

    @pl.when((core == 1) & (k < RUN - 1))
    def _():
        for other in range(2):
            signal(barrier, here(k + 1, other))

    @pl.when(jnp.logical_not(is_late))
    def _():
        signal(barrier, pair)
        for d in range(1, 4):
            signal(barrier, in_plane(turn(x, d), y))
            signal(barrier, in_plane(x, turn(y, d)))

    @pl.when(z_hi == 0)
    def _():
        signal(barrier, antipode)

    @pl.when((z_hi == 0) & (core == 1) & (k == 3))
    def _():
        for source in range(8, 16):
            for other in range(2):
                signal(barrier, here(source, other))

    line = lax.broadcasted_iota(jnp.int32, (16, BLOCK), 0)
    codes = jnp.zeros((16, BLOCK), jnp.int32)
    for slot in range(SLOTS):
        used = slot < p_count[0]
        codes = jnp.where(line == slot, jnp.where(used, p_rows[slot], NO_ROW), codes)
        codes = jnp.where(line == SLOTS + slot, jnp.where(used, p_cols[slot], NO_COL), codes)
    meta[...] = codes.astype(jnp.float32).astype(jnp.bfloat16)
    local(meta, mine_row.at[pl.ds(META, 16)], 2)
    local(meta, mine_col.at[pl.ds(META, 16)], 3)

    expected = (
        flag(k < RUN - 1) + flag(k > 0) + 1 - flag(late_pair) + 6 - flag(late_plane) + flag((z_hi == 0) & (k >= 8)) + z_hi
    )
    pl.semaphore_wait(barrier, expected)

    @pl.when(z_hi == 1)
    def _():
        signal(ready_anti, antipode)

    @pl.when(is_late)
    def _():
        signal(ready_pair, pair)
        for d in range(1, 4):
            signal(ready_pair, in_plane(turn(x, d), y))
            signal(ready_pair, in_plane(x, turn(y, d)))

    for copy in copies:
        copy.wait()

    def send(src, dst, send_sem, recv_sem, target):
        return pltpu.make_async_remote_copy(
            src_ref=src, dst_ref=dst, send_sem=send_sem, recv_sem=recv_sem, device_id=target, device_id_type=MESH
        )

    def pair_send(tile):
        return send(row_tiles.at[tile], row_tiles.at[tile], send_pair.at[tile], row_recv.at[tile, 0], pair)

    def piece_sends(tile, send_sem, target):
        parts = [row_tiles.at[tile, pl.ds(low, size)] for low, size in PIECES]
        return [send(part, part, send_sem.at[n], row_recv.at[tile, n], target) for n, part in enumerate(parts)]

    anti_send = send(mine_col, mine_col, own_sem.at[4], anti_recv, antipode)
    own_sends = (
        (k > 0, piece_sends(col, send_own.at[0], here(k - 1, 1))),
        (k < RUN - 1, piece_sends(col, send_own.at[1], here(k + 1, 0))),
        ((z_hi == 0) & (k >= 8), piece_sends(col, send_own.at[2], here(3, 1))),
    )

    @pl.when(z_hi == 1)
    def _():
        anti_send.start()

    for wanted, sends in own_sends:

        @pl.when(wanted)
        def _(sends=sends):
            for copy in sends:
                copy.start()

    def half_send(side, tile, half, number, target):
        low, size = HALVES[half]
        part = col_tiles.at[tile, pl.ds(low, size)]
        return send(part, part, send_xy.at[side, number], col_recv.at[tile, half], target)

    def plane_tile(side, nx, ny):
        z = z_hi if side == 0 else 1 - z_hi
        return z * 16 + nx * 4 + ny

    def plane_own(side):
        mine = plane_tile(side, x, y)
        return [
            half_send(side, mine, half, number * 6 + (d - 1) * 2 + half, in_plane(turn(x, d), y) if along_x else in_plane(x, turn(y, d)))
            for number in range(2)
            for d in (2, 1, 3)
            for half in range(2)
            for along_x in ((half == 0) == (number == 0),)
        ]

    def plane_forward(side, d):
        from_x = plane_tile(side, turn(x, 4 - d), y)
        from_y = plane_tile(side, x, turn(y, 4 - d))
        first = [half_send(side, from_x, 0, 12 + (d - 1) * 6 + e - 1, in_plane(x, turn(y, e))) for e in (2, 1, 3)]
        second = [half_send(side, from_y, 1, 15 + (d - 1) * 6 + e - 1, in_plane(turn(x, e), y)) for e in (2, 1, 3)]
        return first, second

    def arrived(side, tile, half):
        half_send(side, tile, half, 0, pair).wait_recv()

    def plane_first(side):
        for copy in plane_own(side):
            copy.start()

    def plane_second(side):
        for d in (1, 3, 2):
            first, second = plane_forward(side, d)
            arrived(side, plane_tile(side, turn(x, 4 - d), y), 0)
            for copy in first:
                copy.start()
            arrived(side, plane_tile(side, x, turn(y, 4 - d)), 1)
            for copy in second:
                copy.start()

    def plane_sent(side):
        for copy in plane_own(side):
            copy.wait_send()
        for d in range(1, 4):
            for copies_of in plane_forward(side, d):
                for copy in copies_of:
                    copy.wait_send()

    @pl.when(late_plane)
    def _():
        pl.semaphore_wait(ready_pair, 1)

    plane_first(0)

    @pl.when(late_pair)
    def _():
        pl.semaphore_wait(ready_pair, 1)

    pair_send(col).start()
    plane_second(0)

    step = 2 * core - 1
    onward = here(jnp.clip(k - step, 0, RUN - 1), core)

    def is_valid(source):
        return (source >= 0) & (source < RUN)

    def goes_on(source):
        left = (k > 0) & jnp.logical_not((z_hi == 0) & (k == 4) & (source >= 8))
        return jnp.where(core == 0, flag(k < RUN - 1), flag(left)) == 1

    anti_at, anti_next = 7, 9

    def anti_first():
        @pl.when(z_hi == 0)
        def _():
            pl.semaphore_wait(ready_anti, 1)
            anti_send.start()

        anti_send.wait_recv()
        plane_first(1)

    def stream(t, carry):
        source = k + step * t

        @pl.when(is_valid(source))
        def _():
            goes = goes_on(source)
            for other in range(2):
                tile = source * 2 + other
                for copy in piece_sends(tile, send_row.at[tile], onward):
                    copy.wait_recv()
                    pl.when(goes)(copy.start)
                pair_send(tile).start()

        @pl.when(t == anti_at)
        def _():
            anti_first()

        @pl.when(t == anti_next)
        def _():
            plane_second(1)

        return carry

    lax.fori_loop(1, RUN, stream, 0)

    out[...] = jnp.zeros(out.shape, out.dtype)

    def spread(tiles, tile, number):
        line_of = tiles[tile, pl.ds(META, 16), :].astype(jnp.float32)[number : number + 1, :]
        return jnp.broadcast_to(line_of, (16, BLOCK))

    def weight(condition):
        return jnp.where(condition, 1.0, 0.0).astype(jnp.float32)

    def multiply(n, carry):
        tile = jnp.where(n < 16, z_hi * 16 + n, (1 - z_hi) * 16 + n - 16)
        source, other = tile // 2, tile % 2
        side = flag(n >= 16)
        nx, ny = (tile // 4) % 4, tile % 4
        own_x, own_y = nx == x, ny == y

        @pl.when(((source - k) * step < 0) | ((source == k) & (other != core)))
        def _():
            pair_send(tile).wait_recv()

        @pl.when(jnp.logical_not(own_y))
        def _():
            arrived(side, tile, 0)

        @pl.when(jnp.logical_not(own_x))
        def _():
            arrived(side, tile, 1)

        left_rows = [spread(row_tiles, tile, s) for s in range(SLOTS)]
        left_cols = [spread(row_tiles, tile, SLOTS + s) for s in range(SLOTS)]
        right_rows = [spread(col_tiles, tile, s) for s in range(SLOTS)]
        right_cols = [spread(col_tiles, tile, SLOTS + s) for s in range(SLOTS)]
        inner = [[weight(left_cols[a] == right_rows[b]) for b in range(SLOTS)] for a in range(SLOTS)]
        for o in range(KEPT):
            in_row = [weight(left_rows[a] == kept_rows[o].astype(jnp.float32)) for a in range(SLOTS)]
            in_col = [weight(right_cols[b] == kept_cols[o].astype(jnp.float32)) for b in range(SLOTS)]
            for b in range(SLOTS):
                factors = [(in_row[a] * in_col[b] * inner[a][b]).astype(jnp.bfloat16) for a in range(SLOTS)]
                for low in range(0, BLOCK, 16):
                    terms = [factors[a] * row_tiles[tile, pl.ds(a * BLOCK + low, 16), :] for a in range(SLOTS)]
                    chosen[pl.ds(o * BLOCK + low, 16), pl.ds(b * BLOCK, BLOCK)] = terms[0] + terms[1] + terms[2]
        out[...] += jnp.dot(chosen[...], col_tiles[tile, pl.ds(0, META), :], preferred_element_type=jnp.float32)
        return carry

    lax.fori_loop(0, 32, multiply, 0)

    def settle(t, carry):
        source = k + step * t

        @pl.when(is_valid(source))
        def _():
            goes = goes_on(source)
            for other in range(2):
                tile = source * 2 + other
                for copy in piece_sends(tile, send_row.at[tile], onward):
                    pl.when(goes)(copy.wait_send)
                pair_send(tile).wait_send()

        return carry

    lax.fori_loop(1, RUN, settle, 0)
    plane_sent(0)
    plane_sent(1)
    anti_send.wait_send()
    pair_send(col).wait_send()
    for wanted, sends in own_sends:

        @pl.when(wanted)
        def _(sends=sends):
            for copy in sends:
                copy.wait_send()


def body(p_blocks, p_rows, p_cols, p_count, kept_rows, kept_cols):
    tiles = 32
    scalars = pl.BlockSpec(memory_space=pltpu.SMEM)
    result = pl.pallas_call(
        square_kernel,
        out_shape=jax.ShapeDtypeStruct((KEPT * BLOCK, BLOCK), jnp.float32),
        in_specs=[scalars] * 5 + [pl.BlockSpec(memory_space=pl.ANY)],
        out_specs=pl.BlockSpec(memory_space=pltpu.VMEM),
        scratch_shapes=[
            pltpu.VMEM((tiles, TILE, BLOCK), jnp.bfloat16),
            pltpu.VMEM((tiles, TILE, BLOCK), jnp.bfloat16),
            pltpu.VMEM((KEPT * BLOCK, META), jnp.bfloat16),
            pltpu.VMEM((16, BLOCK), jnp.bfloat16),
            pltpu.SemaphoreType.DMA((tiles, 3)),
            pltpu.SemaphoreType.DMA((tiles, 2)),
            pltpu.SemaphoreType.DMA,
            pltpu.SemaphoreType.DMA((5,)),
            pltpu.SemaphoreType.DMA((3, 3)),
            pltpu.SemaphoreType.DMA((tiles, 3)),
            pltpu.SemaphoreType.DMA((tiles,)),
            pltpu.SemaphoreType.DMA((2, 30)),
            pltpu.SemaphoreType.REGULAR,
            pltpu.SemaphoreType.REGULAR,
        ],
        compiler_params=pltpu.CompilerParams(collective_id=0, has_side_effects=True, vmem_limit_bytes=24 * 2**20),
        name="square_blocks",
    )(
        p_rows.reshape(SLOTS), p_cols.reshape(SLOTS), p_count.reshape(1), kept_rows.reshape(KEPT), kept_cols.reshape(KEPT),
        p_blocks.reshape(META, BLOCK),
    )
    return result.reshape(1, 1, KEPT, BLOCK, BLOCK)


def solution(mesh):
    placed = (
        P("row", "col", None, None, None),
        P("row", "col", None),
        P("row", "col", None),
        P("row", "col"),
        P("row", "col", None),
        P("row", "col", None),
    )
    return jax.shard_map(
        body,
        mesh=mesh,
        in_specs=placed,
        out_specs=P("row", "col", None, None, None),
        check_vma=False,
    )
```

time: 139 us -> 104 us (0.75)
  the two profiles are of different devices: /device:TPU:992 before, /device:TPU:23 now
where the time goes in v2:
time: 104 us
  Pallas kernels  101 us (97%)
  local copies, waits for them, and re-layouts  2.31 us (2%)
    pallas_call x1, Pallas kernels, body(): pl.pallas_call(square_kernel, out_shape=jax.ShapeDtypeStruct((KEPT * BLOC...  101 us
    unnamed x11, local copies, waits for them, and re-layouts  2.31 us

profile of v2, /device:TPU:23, one launch (start us, length us, event | category | flops | bytes accessed | tf_op | source)
XLA Modules:
  0.0 104.2 jit_solution(8797906851610468205)
XLA Ops:
  0.7 0.0 copy-start.4
  0.7 0.0 copy-start.1
  0.7 0.0 copy-start.2
  0.7 0.0 copy-start.3
  0.7 0.6 copy-done.4
  1.3 0.0 copy-done.1
  1.3 0.0 copy-done.2
  1.3 0.0 copy-done.3
  1.4 0.0 copy-start
  1.4 0.9 copy-done
  2.2 101.2 %square_blocks.1 = f32[768,128]{1,0:T(8,128)S(1)} custom-call(s32[3]{0:T(128)S(1)} %bitcast.10, s32[3]{0:T(128)S(1)} %bitcast.11, s32[1]{0:T(128)} %bitcast.7.p_count, s32[6]{0:T(128)S(1)} %bitcast.12, s32[6]{0:T(128)S(1)} %bitcast.13, bf16[384,128]{1,0:T(8,128)(2,1)S(1)} %bitcast.9), custom_call_target="tpu_custom_call" | custom-call | tf_op jit(solution)/shard_map/square_blocks/pallas_call | solution.py:341
  103.4 0.7 copy.9
Async XLA Ops:
  0.7 0.7 copy-start.4
  0.7 0.7 copy-start.1
  0.7 0.7 copy-start.2
  0.7 0.7 copy-start.3
  1.4 0.9 copy-start

commit v3 on v2

--- a/solution.py
+++ b/solution.py
@@ -18,6 +18,7 @@
 PIECES = ((0, 128), (128, 128), (256, TILE - 256))
 RUN = 16
 NO_ROW, NO_COL = 20, 30
+ANTI_T, ANTI_D, READY_T, MULTIPLY_T = 7, 2, 5, 6
 
 
 def device(z_hi, x, y, k, core):
@@ -34,7 +35,7 @@
 
 def square_kernel(
     p_rows, p_cols, p_count, kept_rows, kept_cols, blocks, out,
-    row_tiles, col_tiles, chosen, meta, row_recv, col_recv, anti_recv, own_sem, send_own, send_row, send_pair, send_xy,
+    row_tiles, col_tiles, chosen, meta, row_recv, col_recv, anti_recv, own_sem, send_own, send_anti, send_row, send_pair, send_xy,
     ready_pair, ready_anti,
 ):
     row, col = lax.axis_index("row"), lax.axis_index("col")
@@ -83,15 +84,26 @@
             signal(barrier, in_plane(turn(x, d), y))
             signal(barrier, in_plane(x, turn(y, d)))
 
+    at_end = (k == 0) | (k == RUN - 1)
+    agent = ((k == 0) & (core == 1)) | ((k == RUN - 1) & (core == 0))
+    anti_count = flag(at_end) + 14 * flag(agent)
+    near_end = jnp.where(k < 8, 0, RUN - 1)
+    anti_source = device(1 - z_hi, x, y, near_end, jnp.where(at_end, core, jnp.where(k < 8, 1, 0)))
+    across = functools.partial(device, 1 - z_hi, x, y)
+
     @pl.when(z_hi == 0)
     def _():
-        signal(barrier, antipode)
-
-    @pl.when((z_hi == 0) & (core == 1) & (k == 3))
-    def _():
-        for source in range(8, 16):
-            for other in range(2):
-                signal(barrier, here(source, other))
+        signal(barrier, anti_source)
+
+        @pl.when(at_end)
+        def _():
+            signal(barrier, antipode)
+
+        @pl.when(agent)
+        def _():
+            for distance in range(1, 8):
+                for other in range(2):
+                    signal(barrier, across(jnp.where(core == 1, distance, RUN - 1 - distance), other))
 
     line = lax.broadcasted_iota(jnp.int32, (16, BLOCK), 0)
     codes = jnp.zeros((16, BLOCK), jnp.int32)
@@ -104,13 +116,13 @@
     local(meta, mine_col.at[pl.ds(META, 16)], 3)
 
     expected = (
-        flag(k < RUN - 1) + flag(k > 0) + 1 - flag(late_pair) + 6 - flag(late_plane) + flag((z_hi == 0) & (k >= 8)) + z_hi
+        flag(k < RUN - 1) + flag(k > 0) + 1 - flag(late_pair) + 6 - flag(late_plane) + z_hi * (1 + anti_count)
     )
     pl.semaphore_wait(barrier, expected)
 
     @pl.when(z_hi == 1)
     def _():
-        signal(ready_anti, antipode)
+        signal(ready_anti, anti_source)
 
     @pl.when(is_late)
     def _():
@@ -138,10 +150,9 @@
     own_sends = (
         (k > 0, piece_sends(col, send_own.at[0], here(k - 1, 1))),
         (k < RUN - 1, piece_sends(col, send_own.at[1], here(k + 1, 0))),
-        ((z_hi == 0) & (k >= 8), piece_sends(col, send_own.at[2], here(3, 1))),
     )
 
-    @pl.when(z_hi == 1)
+    @pl.when((z_hi == 1) & at_end)
     def _():
         anti_send.start()
 
@@ -223,44 +234,25 @@
         return (source >= 0) & (source < RUN)
 
     def goes_on(source):
-        left = (k > 0) & jnp.logical_not((z_hi == 0) & (k == 4) & (source >= 8))
-        return jnp.where(core == 0, flag(k < RUN - 1), flag(left)) == 1
-
-    anti_at, anti_next = 7, 9
+        return jnp.where(core == 0, k, RUN - 1 - k) < RUN - 1
+
+    to_end = jnp.where(core == 0, RUN - 1 - k, k)
+    anti_at = jnp.minimum(ANTI_T + to_end // 2, RUN - 2)
+    anti_next = jnp.minimum(anti_at + ANTI_D, RUN - 1)
+
+    def across_send(distance, other):
+        source = k + step * distance
+        tile = source * 2 + other
+        target = across(source, other)
+        return send(row_tiles.at[tile], col_tiles.at[row], send_anti.at[distance * 2 + other], anti_recv, target)
+
+    def across_start(distance):
+        for other in range(2):
+            across_send(distance, other).start()
 
     def anti_first():
-        @pl.when(z_hi == 0)
-        def _():
-            pl.semaphore_wait(ready_anti, 1)
-            anti_send.start()
-
         anti_send.wait_recv()
         plane_first(1)
-
-    def stream(t, carry):
-        source = k + step * t
-
-        @pl.when(is_valid(source))
-        def _():
-            goes = goes_on(source)
-            for other in range(2):
-                tile = source * 2 + other
-                for copy in piece_sends(tile, send_row.at[tile], onward):
-                    copy.wait_recv()
-                    pl.when(goes)(copy.start)
-                pair_send(tile).start()
-
-        @pl.when(t == anti_at)
-        def _():
-            anti_first()
-
-        @pl.when(t == anti_next)
-        def _():
-            plane_second(1)
-
-        return carry
-
-    lax.fori_loop(1, RUN, stream, 0)
 
     out[...] = jnp.zeros(out.shape, out.dtype)
 
@@ -271,16 +263,9 @@
     def weight(condition):
         return jnp.where(condition, 1.0, 0.0).astype(jnp.float32)
 
-    def multiply(n, carry):
-        tile = jnp.where(n < 16, z_hi * 16 + n, (1 - z_hi) * 16 + n - 16)
-        source, other = tile // 2, tile % 2
-        side = flag(n >= 16)
-        nx, ny = (tile // 4) % 4, tile % 4
-        own_x, own_y = nx == x, ny == y
-
-        @pl.when(((source - k) * step < 0) | ((source == k) & (other != core)))
-        def _():
-            pair_send(tile).wait_recv()
+    def multiply(tile):
+        side = flag(tile // 16 != z_hi)
+        own_x, own_y = (tile // 4) % 4 == x, tile % 4 == y
 
         @pl.when(jnp.logical_not(own_y))
         def _():
@@ -304,9 +289,83 @@
                     terms = [factors[a] * row_tiles[tile, pl.ds(a * BLOCK + low, 16), :] for a in range(SLOTS)]
                     chosen[pl.ds(o * BLOCK + low, 16), pl.ds(b * BLOCK, BLOCK)] = terms[0] + terms[1] + terms[2]
         out[...] += jnp.dot(chosen[...], col_tiles[tile, pl.ds(0, META), :], preferred_element_type=jnp.float32)
+
+    def is_early(source, t):
+        return (source // 8 == z_hi) | (t > anti_next + 1)
+
+    def multiply_early(t, number):
+        place = jnp.maximum((t - MULTIPLY_T) * 3 + number, 0)
+        source = k + step * (place // 2 + 1)
+
+        @pl.when((t >= MULTIPLY_T) & is_valid(source) & is_early(source, t))
+        def _():
+            multiply(source * 2 + place % 2)
+
+    def stream(t, carry):
+        source = k + step * t
+
+        def part(other, carry):
+            @pl.when(is_valid(source))
+            def _():
+                goes = goes_on(source)
+                tile = source * 2 + other
+                for copy in piece_sends(tile, send_row.at[tile], onward):
+                    copy.wait_recv()
+                    pl.when(goes)(copy.start)
+                pair_send(tile).start()
+
+            def between(n, carry):
+                multiply_early(t, other + n)
+                return carry
+
+            return lax.fori_loop(0, 1 + other, between, carry)
+
+        lax.fori_loop(0, 2, part, 0)
+
+        @pl.when(agent & (t < 8) & ((z_hi == 1) | (t > READY_T)))
+        def _():
+            across_start(t)
+
+        @pl.when(at_end & (z_hi == 0) & (t == READY_T))
+        def _():
+            pl.semaphore_wait(ready_anti, anti_count)
+            anti_send.start()
+
+            @pl.when(agent)
+            def _():
+                for distance in range(1, READY_T + 1):
+                    across_start(distance)
+
+        @pl.when(t == anti_at)
+        def _():
+            anti_first()
+
+        @pl.when(t == anti_next)
+        def _():
+            plane_second(1)
+
         return carry
 
-    lax.fori_loop(0, 32, multiply, 0)
+    lax.fori_loop(1, RUN, stream, 0)
+
+    def rest(n, carry):
+        tile = jnp.where(n < 16, z_hi * 16 + n, (1 - z_hi) * 16 + n - 16)
+        source, other = tile // 2, tile % 2
+        distance = (source - k) * step
+        by_pair = (distance < 0) | ((distance == 0) & (other != core))
+        done = (distance > 0) & is_early(source, MULTIPLY_T + ((distance - 1) * 2 + other) // 3)
+
+        @pl.when(by_pair)
+        def _():
+            pair_send(tile).wait_recv()
+
+        @pl.when(jnp.logical_not(done))
+        def _():
+            multiply(tile)
+
+        return carry
+
+    lax.fori_loop(0, 32, rest, 0)
 
     def settle(t, carry):
         source = k + step * t
@@ -325,7 +384,14 @@
     lax.fori_loop(1, RUN, settle, 0)
     plane_sent(0)
     plane_sent(1)
-    anti_send.wait_send()
+    pl.when(at_end)(anti_send.wait_send)
+
+    @pl.when(agent)
+    def _():
+        for distance in range(1, 8):
+            for other in range(2):
+                across_send(distance, other).wait_send()
+
     pair_send(col).wait_send()
     for wanted, sends in own_sends:
 
@@ -352,7 +418,8 @@
             pltpu.SemaphoreType.DMA((tiles, 2)),
             pltpu.SemaphoreType.DMA,
             pltpu.SemaphoreType.DMA((5,)),
-            pltpu.SemaphoreType.DMA((3, 3)),
+            pltpu.SemaphoreType.DMA((2, 3)),
+            pltpu.SemaphoreType.DMA((16,)),
             pltpu.SemaphoreType.DMA((tiles, 3)),
             pltpu.SemaphoreType.DMA((tiles,)),
             pltpu.SemaphoreType.DMA((2, 30)),

time: 104 us -> 88.7 us (0.85)
  the two profiles are of different devices: /device:TPU:23 before, /device:TPU:1 now
where the time goes in v3:
time: 88.7 us; the launch traced here: 88.5 us
  Pallas kernels  85.5 us (96%)
  local copies, waits for them, and re-layouts  2.31 us (3%)
    pallas_call x1, Pallas kernels, body(): pl.pallas_call(square_kernel, out_shape=jax.ShapeDtypeStruct((KEPT * BLOC...  85.5 us
    unnamed x11, local copies, waits for them, and re-layouts  2.31 us

profile of v3, /device:TPU:1, one launch (start us, length us, event | category | flops | bytes accessed | tf_op | source)
XLA Modules:
  0.0 88.5 jit_solution(1277796662885848146)
XLA Ops:
  0.7 0.0 copy-start.4
  0.7 0.0 copy-start.1
  0.7 0.0 copy-start.2
  0.7 0.0 copy-start.3
  0.7 0.6 copy-done.4
  1.3 0.0 copy-done.1
  1.3 0.0 copy-done.2
  1.3 0.0 copy-done.3
  1.4 0.0 copy-start
  1.4 0.9 %copy-done = bf16[1,1,3,128,128]{4,3,2,1,0:T(8,128)(2,1)S(1)} copy-done((bf16[1,1,3,128,128]{4,3,2,1,0:T(8,128)(2,1)S(1)}, bf16[1,1,3,128,128]{4,3,2,1,0:T(8,128)(2,1)}, u32[]{:S(2)}) %copy-start) | copy-done | bytes 98328
  2.2 85.5 %square_blocks.1 = f32[768,128]{1,0:T(8,128)S(1)} custom-call(s32[3]{0:T(128)S(1)} %bitcast.10, s32[3]{0:T(128)S(1)} %bitcast.11, s32[1]{0:T(128)} %bitcast.7.p_count, s32[6]{0:T(128)S(1)} %bitcast.12, s32[6]{0:T(128)S(1)} %bitcast.13, bf16[384,128]{1,0:T(8,128)(2,1)S(1)} %bitcast.9), custom_call_target="tpu_custom_call" | custom-call | tf_op jit(solution)/shard_map/square_blocks/pallas_call | solution.py:407
  87.8 0.7 copy.9
Async XLA Ops:
  0.7 0.7 copy-start.4
  0.7 0.7 copy-start.1
  0.7 0.7 copy-start.2
  0.7 0.7 copy-start.3
  1.4 0.9 %copy-start = (bf16[1,1,3,128,128]{4,3,2,1,0:T(8,128)(2,1)S(1)}, bf16[1,1,3,128,128]{4,3,2,1,0:T(8,128)(2,1)}, u32[]{:S(2)}) copy-start(bf16[1,1,3,128,128]{4,3,2,1,0:T(8,128)(2,1)} %param.6) | copy-start | bytes 294916

commit v4 on v3

--- a/solution.py
+++ b/solution.py
@@ -15,10 +15,12 @@
 TILE = META + 16
 HALF = 208
 HALVES = ((0, HALF), (HALF, TILE - HALF))
+NEAR = 3
+RIGHT_FROM = 7
 PIECES = ((0, 128), (128, 128), (256, TILE - 256))
 RUN = 16
 NO_ROW, NO_COL = 20, 30
-ANTI_T, ANTI_D, READY_T, MULTIPLY_T = 7, 2, 5, 6
+ANTI_D, READY_T, MULTIPLY_T = 2, 6, 6
 
 
 def device(z_hi, x, y, k, core):
@@ -86,9 +88,15 @@
 
     at_end = (k == 0) | (k == RUN - 1)
     agent = ((k == 0) & (core == 1)) | ((k == RUN - 1) & (core == 0))
-    anti_count = flag(at_end) + 14 * flag(agent)
-    near_end = jnp.where(k < 8, 0, RUN - 1)
-    anti_source = device(1 - z_hi, x, y, near_end, jnp.where(at_end, core, jnp.where(k < 8, 1, 0)))
+    across_low = jnp.where(z_hi == 0, 8, 1)
+    across_high = jnp.where(z_hi == 0, 14 - NEAR, jnp.where(core == 1, RIGHT_FROM - 1, 15 - RIGHT_FROM))
+    anti_count = flag(at_end) + flag(agent) * 2 * (across_high - across_low + 1 + NEAR * (1 - z_hi))
+    near_left, near_right = k <= NEAR, k >= RUN - 1 - NEAR
+    from_left = jnp.where(z_hi == 0, flag(k < RIGHT_FROM), flag(near_left | ((k >= 8) & jnp.logical_not(near_right)))) == 1
+    anti_source = device(
+        1 - z_hi, x, y,
+        jnp.where(at_end, k, jnp.where(from_left, 0, RUN - 1)), jnp.where(at_end, core, jnp.where(from_left, 1, 0)),
+    )
     across = functools.partial(device, 1 - z_hi, x, y)
 
     @pl.when(z_hi == 0)
@@ -101,7 +109,7 @@
 
         @pl.when(agent)
         def _():
-            for distance in range(1, 8):
+            for distance in (*range(1, NEAR + 1), *range(8, 15 - NEAR)):
                 for other in range(2):
                     signal(barrier, across(jnp.where(core == 1, distance, RUN - 1 - distance), other))
 
@@ -236,8 +244,10 @@
     def goes_on(source):
         return jnp.where(core == 0, k, RUN - 1 - k) < RUN - 1
 
-    to_end = jnp.where(core == 0, RUN - 1 - k, k)
-    anti_at = jnp.minimum(ANTI_T + to_end // 2, RUN - 2)
+    late = RUN - 2
+    run0_at = jnp.where(core == 1, jnp.where(k < RIGHT_FROM, 7 + k // 2, late), jnp.minimum(5 + 2 * (RUN - 1 - k), late))
+    run1_at = jnp.where(at_end, 8, jnp.where(jnp.where(core == 1, flag(near_left), flag(near_right)) == 1, 10, late))
+    anti_at = jnp.where(z_hi == 0, run0_at, run1_at)
     anti_next = jnp.minimum(anti_at + ANTI_D, RUN - 1)
 
     def across_send(distance, other):
@@ -322,10 +332,6 @@
 
         lax.fori_loop(0, 2, part, 0)
 
-        @pl.when(agent & (t < 8) & ((z_hi == 1) | (t > READY_T)))
-        def _():
-            across_start(t)
-
         @pl.when(at_end & (z_hi == 0) & (t == READY_T))
         def _():
             pl.semaphore_wait(ready_anti, anti_count)
@@ -333,8 +339,12 @@
 
             @pl.when(agent)
             def _():
-                for distance in range(1, READY_T + 1):
+                for distance in range(1, NEAR + 1):
                     across_start(distance)
+
+        @pl.when(agent & (t >= across_low) & (t <= across_high))
+        def _():
+            across_start(t)
 
         @pl.when(t == anti_at)
         def _():
@@ -388,9 +398,16 @@
 
     @pl.when(agent)
     def _():
-        for distance in range(1, 8):
+        def across_sent(distance, carry):
             for other in range(2):
                 across_send(distance, other).wait_send()
+            return carry
+
+        lax.fori_loop(across_low, across_high + 1, across_sent, 0)
+
+        @pl.when(z_hi == 0)
+        def _():
+            lax.fori_loop(1, NEAR + 1, across_sent, 0)
 
     pair_send(col).wait_send()
     for wanted, sends in own_sends:
@@ -419,7 +436,7 @@
             pltpu.SemaphoreType.DMA,
             pltpu.SemaphoreType.DMA((5,)),
             pltpu.SemaphoreType.DMA((2, 3)),
-            pltpu.SemaphoreType.DMA((16,)),
+            pltpu.SemaphoreType.DMA((32,)),
             pltpu.SemaphoreType.DMA((tiles, 3)),
             pltpu.SemaphoreType.DMA((tiles,)),
             pltpu.SemaphoreType.DMA((2, 30)),

time: 88.7 us -> 84.7 us (0.955)
  Pallas kernels: 85.5 us -> 81.5 us
    pallas_call x1, Pallas kernels: 85.5 us -> 81.5 us  [body(): pl.pallas_call(square_kernel, out_shape=jax.ShapeDtypeStruct((KEPT * BLOC...]
where the time goes in v4:
time: 84.7 us; the launch traced here: 84.5 us
  Pallas kernels  81.5 us (96%)
  local copies, waits for them, and re-layouts  2.31 us (3%)
    pallas_call x1, Pallas kernels, body(): pl.pallas_call(square_kernel, out_shape=jax.ShapeDtypeStruct((KEPT * BLOC...  81.5 us
    unnamed x11, local copies, waits for them, and re-layouts  2.31 us

profile of v4, /device:TPU:1, one launch (start us, length us, event | category | flops | bytes accessed | tf_op | source)
XLA Modules:
  0.0 84.5 jit_solution(1347373687091309279)
XLA Ops:
  0.7 0.0 copy-start.4
  0.7 0.0 copy-start.1
  0.7 0.0 copy-start.2
  0.7 0.0 copy-start.3
  0.7 0.6 copy-done.4
  1.3 0.0 copy-done.1
  1.3 0.0 copy-done.2
  1.3 0.0 copy-done.3
  1.4 0.0 copy-start
  1.4 0.9 %copy-done = bf16[1,1,3,128,128]{4,3,2,1,0:T(8,128)(2,1)S(1)} copy-done((bf16[1,1,3,128,128]{4,3,2,1,0:T(8,128)(2,1)S(1)}, bf16[1,1,3,128,128]{4,3,2,1,0:T(8,128)(2,1)}, u32[]{:S(2)}) %copy-start) | copy-done | bytes 98328
  2.2 81.5 %square_blocks.1 = f32[768,128]{1,0:T(8,128)S(1)} custom-call(s32[3]{0:T(128)S(1)} %bitcast.10, s32[3]{0:T(128)S(1)} %bitcast.11, s32[1]{0:T(128)} %bitcast.7.p_count, s32[6]{0:T(128)S(1)} %bitcast.12, s32[6]{0:T(128)S(1)} %bitcast.13, bf16[384,128]{1,0:T(8,128)(2,1)S(1)} %bitcast.9), custom_call_target="tpu_custom_call" | custom-call | tf_op jit(solution)/shard_map/square_blocks/pallas_call | solution.py:424
  83.8 0.7 copy.9
Async XLA Ops:
  0.7 0.7 copy-start.4
  0.7 0.7 copy-start.1
  0.7 0.7 copy-start.2
  0.7 0.7 copy-start.3
  1.4 0.9 %copy-start = (bf16[1,1,3,128,128]{4,3,2,1,0:T(8,128)(2,1)S(1)}, bf16[1,1,3,128,128]{4,3,2,1,0:T(8,128)(2,1)}, u32[]{:S(2)}) copy-start(bf16[1,1,3,128,128]{4,3,2,1,0:T(8,128)(2,1)} %param.6) | copy-start | bytes 294916

commit v5 on v4

--- a/solution.py
+++ b/solution.py
@@ -245,7 +245,7 @@
         return jnp.where(core == 0, k, RUN - 1 - k) < RUN - 1
 
     late = RUN - 2
-    run0_at = jnp.where(core == 1, jnp.where(k < RIGHT_FROM, 7 + k // 2, late), jnp.minimum(5 + 2 * (RUN - 1 - k), late))
+    run0_at = jnp.where(core == 1, jnp.where(k < RIGHT_FROM, 6 + k // 2, late), jnp.minimum(5 + 2 * (RUN - 1 - k), late))
     run1_at = jnp.where(at_end, 8, jnp.where(jnp.where(core == 1, flag(near_left), flag(near_right)) == 1, 10, late))
     anti_at = jnp.where(z_hi == 0, run0_at, run1_at)
     anti_next = jnp.minimum(anti_at + ANTI_D, RUN - 1)
@@ -443,7 +443,7 @@
             pltpu.SemaphoreType.REGULAR,
             pltpu.SemaphoreType.REGULAR,
         ],
-        compiler_params=pltpu.CompilerParams(collective_id=0, has_side_effects=True, vmem_limit_bytes=24 * 2**20),
+        compiler_params=pltpu.CompilerParams(collective_id=0, has_side_effects=True, vmem_limit_bytes=60 * 2**20),
         name="square_blocks",
     )(
         p_rows.reshape(SLOTS), p_cols.reshape(SLOTS), p_count.reshape(1), kept_rows.reshape(KEPT), kept_cols.reshape(KEPT),

time: 84.7 us -> 84.2 us (level)
    unnamed x11 -> x1, local copies, waits for them, and re-layouts: 2.31 us -> 1.77 us
where the time goes in v5:
time: 84.2 us; the launch traced here: 83.9 us
  Pallas kernels  81.5 us (97%)
  local copies, waits for them, and re-layouts  1.77 us (2%)
    pallas_call x1, Pallas kernels, body(): pl.pallas_call(square_kernel, out_shape=jax.ShapeDtypeStruct((KEPT * BLOC...  81.5 us
    unnamed x1, local copies, waits for them, and re-layouts  1.77 us

profile of v5, /device:TPU:1, one launch (start us, length us, event | category | flops | bytes accessed | tf_op | source)
XLA Modules:
  0.0 83.9 jit_solution(9874888739826110612)
XLA Ops:
  0.7 81.5 %square_blocks.1 = f32[768,128]{1,0:T(8,128)} custom-call(s32[3]{0:T(128)} %bitcast.10, s32[3]{0:T(128)} %bitcast.11, s32[1]{0:T(128)} %bitcast.7.p_count, s32[6]{0:T(128)} %bitcast.12, s32[6]{0:T(128)} %bitcast.13, bf16[384,128]{1,0:T(8,128)(2,1)} %bitcast.9), custom_call_target="tpu_custom_call" | custom-call | tf_op jit(solution)/shard_map/square_blocks/pallas_call | solution.py:424
  82.2 1.8 %copy.9 = f32[1,1,6,128,128]{4,3,2,1,0:T(8,128)} copy(f32[1,1,6,128,128]{4,3,2,1,0:T(8,128)} %bitcast.8) | data formatting | bytes 786432
